TPU v7x, 32 devices: a whole 2x2x4 slice. The times are simulated.
32 devices in a mesh: case: 2 (over y), lon: 4 (over z), lat: 2 (over x), sub: 2 (over core).
Axes of the slice: x: 2, y: 2, z: 4, core: 2. Of those that a mesh axis runs over, the one named last changes fastest.
Arguments:
- traj_u: float32 [6, 128, 2048], P('case', ('lat', 'sub'), 'lon'), parts along dimension 0, may hold values from -4 to 4
- traj_v: float32 [6, 128, 2048], P('case', ('lat', 'sub'), 'lon'), parts along dimension 0, may hold values from -4 to 4
- adj_h: float32 [16, 128, 2048], P('case', ('lat', 'sub'), 'lon'), parts along dimension 0, may hold values from -6 to 6
- adj_u: float32 [16, 128, 2048], P('case', ('lat', 'sub'), 'lon'), parts along dimension 0, may hold values from -6 to 6
- adj_v: float32 [16, 128, 2048], P('case', ('lat', 'sub'), 'lon'), parts along dimension 0, may hold values from -6 to 6
- depth: float32 [128, 2048], P(('lat', 'sub'), 'lon'), may hold values from 0.25 to 1
- drag: float32 [128, 2048], P(('lat', 'sub'), 'lon'), may hold values from 0.1 to 1
- land: int32 [128, 2048], P(('lat', 'sub'), 'lon'), may hold values 0 or 1
- wet_u: int32 [6, 128, 2048], P('case', ('lat', 'sub'), 'lon'), parts along dimension 0, may hold values 0 or 1
- wet_v: int32 [6, 128, 2048], P('case', ('lat', 'sub'), 'lon'), parts along dimension 0, may hold values 0 or 1
Outputs:
- out_h: float32 [16, 128, 2048], P('case', ('lat', 'sub'), 'lon'), parts along dimension 0
- out_u: float32 [16, 128, 2048], P('case', ('lat', 'sub'), 'lon'), parts along dimension 0
- out_v: float32 [16, 128, 2048], P('case', ('lat', 'sub'), 'lon'), parts along dimension 0
- out_depth: float32 [16, 128, 2048], P('case', ('lat', 'sub'), 'lon'), parts along dimension 0
- out_drag: float32 [16, 128, 2048], P('case', ('lat', 'sub'), 'lon'), parts along dimension 0
There are 2 independent parts, one for each index of `case`. A program takes and returns all parts, laid end to end along the dimension named above; an argument that names none is the same for every part. Nothing has to cross between parts.
All inputs are finite; a program needn't handle non-finite values. No bound on the sum of `land` or of `wet_u` or of `wet_v` on one device may be relied on, other than what follows from the above.
Results may differ from a plain program's by a relative error of at most 0.00002.
Values sent between devices are 32-bit elements; how exact they have to be, the bound alone decides.
No kernel may reach another device: no remote copies, remote signals or barrier semaphores. Data moves between devices by JAX's collectives and lax.ppermute only.
A program may use at most 64 MiB of HBM per device.

v0:
```python
import jax
import jax.numpy as jnp
from jax import lax
from jax.sharding import PartitionSpec as P

time_step = 0.5
gravity = 1.0
speed_floor = 0.01


def partner(block, axis, distance):
    count = lax.axis_size(axis)
    route = []
    for low in range(count):
        high = low | 1 << distance
        if high != low and high < count:
            route += [(low, high), (high, low)]
    return lax.ppermute(block, axis, route)


def shifted(value, axis, steps):
    count = lax.axis_size(axis)
    pairs = [(source, (source + steps) % count) for source in range(count)]
    return lax.ppermute(value, axis, pairs)


def passed_along(value, axis, steps):
    count = lax.axis_size(axis)
    leading, last = (max(0, -steps), min(count, count - steps))
    return lax.ppermute(value, axis, [(source, source + steps) for source in range(leading, last)])


def mirror_row(row):
    bit_count = lax.axis_size("lon").bit_length() - 1
    bit_order = list(range(bit_count))
    for bit_number in bit_order:
        row = partner(row, "lon", bit_number)
    return row[..., ::-1]


def continuity(height, flux_u, flux_v, west_col, south_row, fold_row, land_f, at_top):
    west_all = jnp.concatenate([west_col, flux_u[..., :-1]], axis=-1)
    south_all = jnp.concatenate([south_row, flux_v[..., :-1, :]], axis=-2)
    fold_part = jnp.where(at_top, fold_row, jnp.zeros_like(fold_row))
    fold_all = jnp.concatenate([jnp.zeros_like(flux_v[..., :-1, :]), fold_part], axis=-2)
    return height - time_step * land_f * (flux_u - west_all + flux_v - south_all - fold_all)


def momentum(
    height_new,
    east_col,
    north_row,
    fold_row,
    vel_u,
    vel_v,
    depth_u,
    depth_v,
    drag,
    mask_u,
    mask_v,
    at_top,
):
    east_height = jnp.concatenate([height_new[..., 1:], east_col], axis=-1)
    top_row = jnp.where(at_top, fold_row, north_row)
    north_height = jnp.concatenate([height_new[..., 1:, :], top_row], axis=-2)
    drag_u = drag * vel_u * jnp.sqrt(vel_u * vel_u + speed_floor) / depth_u
    drag_v = drag * vel_v * jnp.sqrt(vel_v * vel_v + speed_floor) / depth_v
    u_new = mask_u * (vel_u - time_step * gravity * (east_height - height_new) - time_step * drag_u)
    v_new = mask_v * (
        vel_v - time_step * gravity * (north_height - height_new) - time_step * drag_v
    )
    return (u_new, v_new)


def depth_grad(face_u, face_v, at_top):
    from_west = shifted(face_u[..., -1:], "lon", 1)
    from_south = passed_along(face_v[..., -1:, :], ("lat", "sub"), 1)
    top_part = jnp.where(at_top, face_v[..., -1:, :], jnp.zeros_like(from_south))
    from_fold = mirror_row(top_part)
    west_all = jnp.concatenate([from_west, face_u[..., :-1]], axis=-1)
    south_all = jnp.concatenate([from_south, face_v[..., :-1, :]], axis=-2)
    total = 0.5 * (face_u + face_v + west_all + south_all)
    total = total.at[..., -1:, :].add(0.5 * from_fold)
    return total


def on_device(traj_u, traj_v, adj_h, adj_u, adj_v, depth, drag, land, wet_u, wet_v):
    at_top = lax.axis_index(("lat", "sub")) == lax.axis_size(("lat", "sub")) - 1
    land_f = land.astype(jnp.float32)
    east_depth = shifted(depth[:, :1], "lon", -1)
    north_depth = passed_along(depth[:1, :], ("lat", "sub"), -1)
    fold_depth = mirror_row(depth[-1:, :])
    depth_u = 0.5 * (depth + jnp.concatenate([depth[:, 1:], east_depth], axis=1))
    depth_v = 0.5 * (
        depth + jnp.concatenate([depth[1:], jnp.where(at_top, fold_depth, north_depth)], axis=0)
    )
    shape_all = adj_h.shape

    def spread(field):
        return jnp.broadcast_to(field, shape_all)

    zero_field = jnp.zeros(shape_all, jnp.float32)
    zero_col = zero_field[..., :1]
    zero_row = zero_field[..., :1, :]
    bar_h, bar_u, bar_v = (adj_h, adj_u, adj_v)
    grad_depth = zero_field
    grad_drag = zero_field
    for step_index in range(traj_u.shape[0] - 1, -1, -1):
        mask_u = wet_u[step_index].astype(jnp.float32)
        mask_v = wet_v[step_index].astype(jnp.float32)
        vel_u = spread(traj_u[step_index])
        vel_v = spread(traj_v[step_index])

        def local_momentum(
            height_new,
            east_col,
            north_row,
            fold_row,
            vel_u_in,
            vel_v_in,
            depth_u_in,
            depth_v_in,
            drag_in,
        ):
            return momentum(
                height_new,
                east_col,
                north_row,
                fold_row,
                vel_u_in,
                vel_v_in,
                depth_u_in,
                depth_v_in,
                drag_in,
                mask_u,
                mask_v,
                at_top,
            )

        _, pull_momentum = jax.vjp(
            local_momentum,
            zero_field,
            zero_col,
            zero_row,
            zero_row,
            vel_u,
            vel_v,
            spread(depth_u),
            spread(depth_v),
            spread(drag),
        )
        bar_hn, bar_east, bar_north, bar_fold, moment_u, moment_v, step_du, step_dv, step_drag = (
            pull_momentum((bar_u, bar_v))
        )
        bar_hn = bar_hn + bar_h
        bar_hn = bar_hn.at[..., :1].add(shifted(bar_east, "lon", 1))
        bar_hn = bar_hn.at[..., :1, :].add(passed_along(bar_north, ("lat", "sub"), 1))
        bar_hn = bar_hn.at[..., -1:, :].add(mirror_row(bar_fold))

        def local_continuity(height, flux_u, flux_v, west_col, south_row, fold_row):
            return continuity(height, flux_u, flux_v, west_col, south_row, fold_row, land_f, at_top)

        _, pull_continuity = jax.vjp(
            local_continuity, zero_field, zero_field, zero_field, zero_col, zero_row, zero_row
        )
        bar_h, bar_fu, bar_fv, bar_west, bar_south, bar_fold_flux = pull_continuity(bar_hn)
        bar_fu = bar_fu.at[..., -1:].add(shifted(bar_west, "lon", -1))
        bar_fv = bar_fv.at[..., -1:, :].add(passed_along(bar_south, ("lat", "sub"), -1))
        bar_fv = bar_fv.at[..., -1:, :].add(mirror_row(bar_fold_flux))
        bar_u = moment_u + depth_u * bar_fu
        bar_v = moment_v + depth_v * bar_fv
        step_du = step_du + vel_u * bar_fu
        step_dv = step_dv + vel_v * bar_fv
        grad_drag = grad_drag + step_drag
        grad_depth = grad_depth + depth_grad(step_du, step_dv, at_top)
    return (bar_h, bar_u, bar_v, grad_depth, grad_drag)


def solution(mesh):
    placed = (
        P("case", ("lat", "sub"), "lon"),
        P("case", ("lat", "sub"), "lon"),
        P("case", ("lat", "sub"), "lon"),
        P("case", ("lat", "sub"), "lon"),
        P("case", ("lat", "sub"), "lon"),
        P(("lat", "sub"), "lon"),
        P(("lat", "sub"), "lon"),
        P(("lat", "sub"), "lon"),
        P("case", ("lat", "sub"), "lon"),
        P("case", ("lat", "sub"), "lon"),
    )
    return jax.shard_map(
        on_device,
        mesh=mesh,
        in_specs=placed,
        out_specs=(
            P("case", ("lat", "sub"), "lon"),
            P("case", ("lat", "sub"), "lon"),
            P("case", ("lat", "sub"), "lon"),
            P("case", ("lat", "sub"), "lon"),
            P("case", ("lat", "sub"), "lon"),
        ),
        check_vma=False,
    )
```

profile of v0, /device:TPU:0, one launch (start us, length us, event | category | flops | bytes accessed | tf_op | source)
XLA Modules:
  0.0 167.3 jit_solution(16393933793566569236)
XLA Ops:
  2.7 3.1 %collective-permute-start = (f32[1,512]{1,0:T(1,128)S(1)}, f32[1,512]{1,0:T(1,128)S(1)}, u32[]{:S(2)}, u32[]{:S(2)}) collective-permute-start(f32[1,512]{1,0:T(1,128)S(1)} %get-tuple-element.365), channel_id=1, source_target_pairs={{0,4},{4,0},{8,12},{12,8},{1,5},{5,1},{9,13},{13,9},{2,6},{6,2},{1... | collective-permute-start | bytes 6152 | tf_op jit(solution)/shard_map/ppermute | solution.py:18
  6.5 2.5 %collective-permute-start.10 = (f32[32,1]{1,0:T(8,128)S(1)}, f32[32,1]{1,0:T(8,128)S(1)}, u32[]{:S(2)}, u32[]{:S(2)}) collective-permute-start(f32[32,1]{1,0:T(8,128)S(1)} %slice.604), channel_id=1, source_target_pairs={{0,12},{4,0},{8,4},{12,8},{1,13},{5,1},{9,5},{13,9},{2,14},{6,2},{... | collective-permute-start | bytes 392 | tf_op jit(solution)/shard_map/ppermute | solution.py:24
  16.6 2.3 %collective-permute-done.3 = f32[8,32,1]{2,1,0:T(8,128)S(1)} collective-permute-done((f32[8,32,1]{2,1,0:T(8,128)S(1)}, f32[8,32,1]{2,1,0:T(8,128)S(1)}, u32[]{:S(2)}, u32[]{:S(2)}) %collective-permute-start.3) | collective-permute-done | bytes 1056 | tf_op jit(solution)/shard_map/ppermute | solution.py:24
  21.5 3.4 %collective-permute-done.1 = f32[1,512]{1,0:T(1,128)S(1)} collective-permute-done((f32[1,512]{1,0:T(1,128)S(1)}, f32[1,512]{1,0:T(1,128)S(1)}, u32[]{:S(2)}, u32[]{:S(2)}) %collective-permute-start.1) | collective-permute-done | bytes 2080 | tf_op jit(solution)/shard_map/ppermute | solution.py:18
  27.1 3.7 %collective-permute-done.6 = f32[8,1,512]{2,1,0:T(1,128)S(1)} collective-permute-done((f32[8,1,512]{2,1,0:T(1,128)S(1)}, f32[8,1,512]{2,1,0:T(1,128)S(1)}, u32[]{:S(2)}, u32[]{:S(2)}) %collective-permute-start.6) | collective-permute-done | bytes 16416 | tf_op jit(solution)/shard_map/ppermute | solution.py:18
  33.7 2.3 %collective-permute-start.11 = (f32[8,32,1]{2,1,0:T(8,128)S(1)}, f32[8,32,1]{2,1,0:T(8,128)S(1)}, u32[]{:S(2)}, u32[]{:S(2)}) collective-permute-start(f32[8,32,1]{2,1,0:T(8,128)S(1)} %split.116), channel_id=1, source_target_pairs={{0,12},{4,0},{8,4},{12,8},{1,13},{5,1},{9,5},{13,9},{2,14},{6,2},{... | collective-permute-start | bytes 3080 | tf_op jit(solution)/shard_map/ppermute | solution.py:24
  37.1 3.4 %collective-permute-done.11 = f32[8,32,1]{2,1,0:T(8,128)S(1)} collective-permute-done((f32[8,32,1]{2,1,0:T(8,128)S(1)}, f32[8,32,1]{2,1,0:T(8,128)S(1)}, u32[]{:S(2)}, u32[]{:S(2)}) %collective-permute-start.11) | collective-permute-done | bytes 1056 | tf_op jit(solution)/shard_map/ppermute | solution.py:24
  45.9 2.8 %collective-permute-start.28 = (f32[8,32,1]{2,1,0:T(8,128)}, f32[8,32,1]{2,1,0:T(8,128)}, u32[]{:S(2)}, u32[]{:S(2)}) collective-permute-start(f32[8,32,1]{2,1,0:T(8,128)} %slice.650), channel_id=1, source_target_pairs={{0,4},{4,8},{8,12},{12,0},{1,5},{5,9},{9,13},{13,1},{2,6},{6,10},{... | collective-permute-start | bytes 3080 | tf_op jit(solution)/shard_map/ppermute | solution.py:24
  62.7 4.0 %collective-permute-start.29 = (f32[8,1,512]{2,1,0:T(1,128)}, f32[8,1,512]{2,1,0:T(1,128)S(1)}, u32[]{:S(2)}, u32[]{:S(2)}) collective-permute-start(f32[8,1,512]{2,1,0:T(1,128)} %get-tuple-element.301), channel_id=1, source_target_pairs={{0,1},{1,2},{2,3},{4,5},{5,6},{6,7},{8,9},{9,10},{10,11},{12,13},{... | collective-permute-start | bytes 49160 | tf_op jit(solution)/shard_map/ppermute | solution.py:30
  69.3 2.7 %collective-permute-start.15 = (f32[8,1,512]{2,1,0:T(1,128)}, f32[8,1,512]{2,1,0:T(1,128)}, u32[]{:S(2)}, u32[]{:S(2)}) collective-permute-start(f32[8,1,512]{2,1,0:T(1,128)} %collective-permute-done.14), channel_id=1, source_target_pairs={{0,8},{8,0},{4,12},{12,4},{1,9},{9,1},{5,13},{13,5},{2,10},{10,2},... | collective-permute-start | bytes 49160 | tf_op jit(solution)/shard_map/ppermute | solution.py:18
  72.3 2.4 %fusion.17 = f32[8,32,512]{2,1,0:T(8,128)} fusion(f32[8,32,511]{2,1,0:T(8,128)S(1)} %bitcast.92, f32[8,32,1]{2,1,0:T(8,128)} %collective-permute-done.28, f32[8,31,512]{2,1,0:T(8,128)} %bitcast.95, f32[8,1,512]{2,1,0:T(1,128)S(1)} %collective-permute-done.29, f32[8,32,512]{2,1,0:T(8,128)S(1)} %copy-done.10, f32[8,32,512]{2,1,0:T(8,128)} %copy-done.11), kind=kLoop, calls=%fused_computation.24 | loop fusion | flops 786432 | bytes 2621440 | tf_op jit(solution)/shard_map/mul | solution.py:82
  81.9 2.6 %collective-permute-start.19 = (f32[8,32,1]{2,1,0:T(8,128)}, f32[8,32,1]{2,1,0:T(8,128)}, u32[]{:S(2)}, u32[]{:S(2)}) collective-permute-start(f32[8,32,1]{2,1,0:T(8,128)} %split.125), channel_id=1, source_target_pairs={{0,12},{4,0},{8,4},{12,8},{1,13},{5,1},{9,5},{13,9},{2,14},{6,2},{... | collective-permute-start | bytes 3080 | tf_op jit(solution)/shard_map/ppermute | solution.py:24
  92.2 2.7 %rev.34 = f32[8,1,512]{2,1,0:T(1,128)} reverse(f32[8,1,512]{2,1,0:T(1,128)} %collective-permute-done.18), dimensions={2} | reverse | bytes 32768 | tf_op jit(solution)/shard_map/rev | solution.py:38
  99.7 3.3 %add_add_fusion.6 = (f32[8,32,512]{2,1,0:T(8,128)}, f32[8,32,512]{2,1,0:T(8,128)S(1)}, f32[8,32,512]{2,1,0:T(8,128)S(1)}) fusion(f32[32,512]{1,0:T(8,128)} %get-tuple-element.327, f32[32,512]{1,0:T(8,128)} %get-tuple-element.369, f32[32,512]{1,0:T(8,128)} %get-tuple-element.352, f32[32,512]{1,0:T(8,128)} %get-tuple-element.347, ...), kind=kLoop, calls=%fused_computation.31 | loop fusion | flops 7471104 | bytes 6225920 | tf_op jit(solution)/shard_map/add | solution.py:174
  104.8 2.3 %collective-permute-start.21 = (f32[8,1,512]{2,1,0:T(1,128)}, f32[8,1,512]{2,1,0:T(1,128)}, u32[]{:S(2)}, u32[]{:S(2)}) collective-permute-start(f32[8,1,512]{2,1,0:T(1,128)} %get-tuple-element.307), channel_id=1, source_target_pairs={{0,1},{1,2},{2,3},{4,5},{5,6},{6,7},{8,9},{9,10},{10,11},{12,13},{... | collective-permute-start | bytes 49160 | tf_op jit(solution)/shard_map/ppermute | solution.py:30
  108.4 6.7 %collective-permute-done.20 = f32[8,32,1]{2,1,0:T(8,128)S(1)} collective-permute-done((f32[8,32,1]{2,1,0:T(8,128)S(1)}, f32[8,32,1]{2,1,0:T(8,128)S(1)}, u32[]{:S(2)}, u32[]{:S(2)}) %collective-permute-start.20) | collective-permute-done | bytes 1056 | tf_op jit(solution)/shard_map/ppermute | solution.py:24
  117.8 2.5 %collective-permute-done.23 = f32[8,1,512]{2,1,0:T(1,128)S(1)} collective-permute-done((f32[8,1,512]{2,1,0:T(1,128)}, f32[8,1,512]{2,1,0:T(1,128)S(1)}, u32[]{:S(2)}, u32[]{:S(2)}) %collective-permute-start.23) | collective-permute-done | bytes 16416 | tf_op jit(solution)/shard_map/ppermute | solution.py:18
  123.3 3.0 %collective-permute-start.24 = (f32[8,32,1]{2,1,0:T(8,128)S(1)}, f32[8,32,1]{2,1,0:T(8,128)S(1)}, u32[]{:S(2)}, u32[]{:S(2)}) collective-permute-start(f32[8,32,1]{2,1,0:T(8,128)S(1)} %split.131), channel_id=1, source_target_pairs={{0,12},{4,0},{8,4},{12,8},{1,13},{5,1},{9,5},{13,9},{2,14},{6,2},{... | collective-permute-start | bytes 3080 | tf_op jit(solution)/shard_map/ppermute | solution.py:24
  127.3 2.8 %collective-permute-done.24 = f32[8,32,1]{2,1,0:T(8,128)S(1)} collective-permute-done((f32[8,32,1]{2,1,0:T(8,128)S(1)}, f32[8,32,1]{2,1,0:T(8,128)S(1)}, u32[]{:S(2)}, u32[]{:S(2)}) %collective-permute-start.24) | collective-permute-done | bytes 1056 | tf_op jit(solution)/shard_map/ppermute | solution.py:24
  130.2 2.3 %scatter-add.95 = f32[8,32,512]{2,1,0:T(8,128)} dynamic-update-slice(f32[8,32,512]{2,1,0:T(8,128)} %copy-done.13, f32[8,32,1]{2,1,0:T(8,128)S(1)} %slice_add_fusion, s32[]{:T(128)} %constant.473.clone.1, s32[]{:T(128)} %constant.473.clone.1, s32[]{:T(128)} %constant.475.clone.1) | dynamic-update-slice | bytes 2052 | tf_op jit(solution)/shard_map/scatter-add | solution.py:167
  134.1 2.3 %multiply_add_fusion.1 = (f32[8,32,512]{2,1,0:T(8,128)S(1)}, f32[8,32,512]{2,1,0:T(8,128)}, f32[8,32,512]{2,1,0:T(8,128)S(1)}) fusion(f32[8,32,512]{2,1,0:T(8,128)} %scatter-add.95, f32[8,32,512]{2,1,0:T(8,128)S(1)} %copy-done.3, f32[32,512]{1,0:T(8,128)} %get-tuple-element.360, f32[32,512]{1,0:T(8,128)} %get-tuple-element.362, f32[32,512]{1,0:T(8,128)S(1)} %copy-done.23, ...), kind=kLoop, calls=%fused_computation.33 | loop fusion | flops 3145728 | bytes 4325376 | tf_op jit(solution)/shard_map/add | solution.py:172
  138.0 3.3 %collective-permute-start.32 = (f32[8,32,1]{2,1,0:T(8,128)}, f32[8,32,1]{2,1,0:T(8,128)}, u32[]{:S(2)}, u32[]{:S(2)}) collective-permute-start(f32[8,32,1]{2,1,0:T(8,128)} %slice.655), channel_id=1, source_target_pairs={{0,4},{4,8},{8,12},{12,0},{1,5},{5,9},{9,13},{13,1},{2,6},{6,10},{... | collective-permute-start | bytes 3080 | tf_op jit(solution)/shard_map/ppermute | solution.py:24
  147.3 2.6 %multiply_add_fusion = (f32[8,32,512]{2,1,0:T(8,128)S(1)}, f32[8,32,512]{2,1,0:T(8,128)}, f32[8,32,512]{2,1,0:T(8,128)S(1)}) fusion(f32[8,32,512]{2,1,0:T(8,128)} %scatter-add.99, f32[8,32,512]{2,1,0:T(8,128)S(1)} %get-tuple-element.258, f32[32,512]{1,0:T(8,128)} %get-tuple-element.270, f32[32,512]{1,0:T(8,128)S(1)} %copy-done.25, ...), kind=kLoop, calls=%fused_computation.32 | loop fusion | flops 3145728 | bytes 4325376 | tf_op jit(solution)/shard_map/add | solution.py:173
  156.1 2.7 %collective-permute-start.37 = (f32[8,1,512]{2,1,0:T(1,128)S(1)}, f32[8,1,512]{2,1,0:T(1,128)S(1)}, u32[]{:S(2)}, u32[]{:S(2)}) collective-permute-start(f32[8,1,512]{2,1,0:T(1,128)S(1)} %get-tuple-element.303), channel_id=1, source_target_pairs={{0,1},{1,2},{2,3},{4,5},{5,6},{6,7},{8,9},{9,10},{10,11},{12,13},{... | collective-permute-start | bytes 49160 | tf_op jit(solution)/shard_map/ppermute | solution.py:30
  (217 shorter events, 94.2 us)
Async XLA Ops:
  1.4 23.9 %collective-permute-start.2 = (f32[1,512]{1,0:T(1,128)S(1)}, f32[1,512]{1,0:T(1,128)S(1)}, u32[]{:S(2)}, u32[]{:S(2)}) collective-permute-start(f32[1,512]{1,0:T(1,128)S(1)} %get-tuple-element.364), channel_id=1, source_target_pairs={{1,0},{2,1},{3,2},{5,4},{6,5},{7,6},{9,8},{10,9},{11,10},{13,12},{... | collective-permute-start | bytes 6152 | tf_op jit(solution)/shard_map/ppermute | solution.py:30
  2.7 17.7 %collective-permute-start = (f32[1,512]{1,0:T(1,128)S(1)}, f32[1,512]{1,0:T(1,128)S(1)}, u32[]{:S(2)}, u32[]{:S(2)}) collective-permute-start(f32[1,512]{1,0:T(1,128)S(1)} %get-tuple-element.365), channel_id=1, source_target_pairs={{0,4},{4,0},{8,12},{12,8},{1,5},{5,1},{9,13},{13,9},{2,6},{6,2},{1... | collective-permute-start | bytes 6152 | tf_op jit(solution)/shard_map/ppermute | solution.py:18
  6.5 18.8 %collective-permute-start.10 = (f32[32,1]{1,0:T(8,128)S(1)}, f32[32,1]{1,0:T(8,128)S(1)}, u32[]{:S(2)}, u32[]{:S(2)}) collective-permute-start(f32[32,1]{1,0:T(8,128)S(1)} %slice.604), channel_id=1, source_target_pairs={{0,12},{4,0},{8,4},{12,8},{1,13},{5,1},{9,5},{13,9},{2,14},{6,2},{... | collective-permute-start | bytes 392 | tf_op jit(solution)/shard_map/ppermute | solution.py:24
  11.9 14.2 %collective-permute-start.5 = (f32[8,1,512]{2,1,0:T(1,128)S(1)}, f32[8,1,512]{2,1,0:T(1,128)S(1)}, u32[]{:S(2)}, u32[]{:S(2)}) collective-permute-start(f32[8,1,512]{2,1,0:T(1,128)S(1)} %get-tuple-element.314), channel_id=1, source_target_pairs={{0,4},{4,0},{8,12},{12,8},{1,5},{5,1},{9,13},{13,9},{2,6},{6,2},{1... | collective-permute-start | bytes 49160 | tf_op jit(solution)/shard_map/ppermute | solution.py:18
  32.3 18.1 %collective-permute-start.7 = (f32[8,1,512]{2,1,0:T(1,128)}, f32[8,1,512]{2,1,0:T(1,128)S(1)}, u32[]{:S(2)}, u32[]{:S(2)}) collective-permute-start(f32[8,1,512]{2,1,0:T(1,128)} %get-tuple-element.312), channel_id=1, source_target_pairs={{1,0},{2,1},{3,2},{5,4},{6,5},{7,6},{9,8},{10,9},{11,10},{13,12},{... | collective-permute-start | bytes 49160 | tf_op jit(solution)/shard_map/ppermute | solution.py:30
  45.9 26.4 %collective-permute-start.28 = (f32[8,32,1]{2,1,0:T(8,128)}, f32[8,32,1]{2,1,0:T(8,128)}, u32[]{:S(2)}, u32[]{:S(2)}) collective-permute-start(f32[8,32,1]{2,1,0:T(8,128)} %slice.650), channel_id=1, source_target_pairs={{0,4},{4,8},{8,12},{12,0},{1,5},{5,9},{9,13},{13,1},{2,6},{6,10},{... | collective-permute-start | bytes 3080 | tf_op jit(solution)/shard_map/ppermute | solution.py:24
  48.7 14.1 %collective-permute-start.12 = (f32[8,32,1]{2,1,0:T(8,128)}, f32[8,32,1]{2,1,0:T(8,128)}, u32[]{:S(2)}, u32[]{:S(2)}) collective-permute-start(f32[8,32,1]{2,1,0:T(8,128)} %split.119), channel_id=1, source_target_pairs={{0,4},{4,8},{8,12},{12,0},{1,5},{5,9},{9,13},{13,1},{2,6},{6,10},{... | collective-permute-start | bytes 3080 | tf_op jit(solution)/shard_map/ppermute | solution.py:24
  56.8 12.5 %collective-permute-start.14 = (f32[8,1,512]{2,1,0:T(1,128)}, f32[8,1,512]{2,1,0:T(1,128)}, u32[]{:S(2)}, u32[]{:S(2)}) collective-permute-start(f32[8,1,512]{2,1,0:T(1,128)} %get-tuple-element.310), channel_id=1, source_target_pairs={{0,4},{4,0},{8,12},{12,8},{1,5},{5,1},{9,13},{13,9},{2,6},{6,2},{1... | collective-permute-start | bytes 49160 | tf_op jit(solution)/shard_map/ppermute | solution.py:18
  57.6 17.1 %collective-permute-start.13 = (f32[8,1,512]{2,1,0:T(1,128)}, f32[8,1,512]{2,1,0:T(1,128)}, u32[]{:S(2)}, u32[]{:S(2)}) collective-permute-start(f32[8,1,512]{2,1,0:T(1,128)} %get-tuple-element.311), channel_id=1, source_target_pairs={{0,1},{1,2},{2,3},{4,5},{5,6},{6,7},{8,9},{9,10},{10,11},{12,13},{... | collective-permute-start | bytes 49160 | tf_op jit(solution)/shard_map/ppermute | solution.py:30
  60.1 11.9 %collective-permute-start.30 = (f32[8,1,512]{2,1,0:T(1,128)}, f32[8,1,512]{2,1,0:T(1,128)}, u32[]{:S(2)}, u32[]{:S(2)}) collective-permute-start(f32[8,1,512]{2,1,0:T(1,128)} %get-tuple-element.300), channel_id=1, source_target_pairs={{0,4},{4,0},{8,12},{12,8},{1,5},{5,1},{9,13},{13,9},{2,6},{6,2},{1... | collective-permute-start | bytes 49160 | tf_op jit(solution)/shard_map/ppermute | solution.py:18
  62.7 9.6 %collective-permute-start.29 = (f32[8,1,512]{2,1,0:T(1,128)}, f32[8,1,512]{2,1,0:T(1,128)S(1)}, u32[]{:S(2)}, u32[]{:S(2)}) collective-permute-start(f32[8,1,512]{2,1,0:T(1,128)} %get-tuple-element.301), channel_id=1, source_target_pairs={{0,1},{1,2},{2,3},{4,5},{5,6},{6,7},{8,9},{9,10},{10,11},{12,13},{... | collective-permute-start | bytes 49160 | tf_op jit(solution)/shard_map/ppermute | solution.py:30
  72.0 13.5 %collective-permute-start.31 = (f32[8,1,512]{2,1,0:T(1,128)}, f32[8,1,512]{2,1,0:T(1,128)}, u32[]{:S(2)}, u32[]{:S(2)}) collective-permute-start(f32[8,1,512]{2,1,0:T(1,128)} %collective-permute-done.30), channel_id=1, source_target_pairs={{0,8},{8,0},{4,12},{12,4},{1,9},{9,1},{5,13},{13,5},{2,10},{10,2},... | collective-permute-start | bytes 49160 | tf_op jit(solution)/shard_map/ppermute | solution.py:18
  79.1 15.9 %collective-permute-start.16 = (f32[8,1,512]{2,1,0:T(1,128)}, f32[8,1,512]{2,1,0:T(1,128)}, u32[]{:S(2)}, u32[]{:S(2)}) collective-permute-start(f32[8,1,512]{2,1,0:T(1,128)} %get-tuple-element.308), channel_id=1, source_target_pairs={{1,0},{2,1},{3,2},{5,4},{6,5},{7,6},{9,8},{10,9},{11,10},{13,12},{... | collective-permute-start | bytes 49160 | tf_op jit(solution)/shard_map/ppermute | solution.py:30
  103.8 11.5 %collective-permute-start.22 = (f32[8,1,512]{2,1,0:T(1,128)}, f32[8,1,512]{2,1,0:T(1,128)}, u32[]{:S(2)}, u32[]{:S(2)}) collective-permute-start(f32[8,1,512]{2,1,0:T(1,128)} %get-tuple-element.306), channel_id=1, source_target_pairs={{0,4},{4,0},{8,12},{12,8},{1,5},{5,1},{9,13},{13,9},{2,6},{6,2},{1... | collective-permute-start | bytes 49160 | tf_op jit(solution)/shard_map/ppermute | solution.py:18
  104.8 12.2 %collective-permute-start.21 = (f32[8,1,512]{2,1,0:T(1,128)}, f32[8,1,512]{2,1,0:T(1,128)}, u32[]{:S(2)}, u32[]{:S(2)}) collective-permute-start(f32[8,1,512]{2,1,0:T(1,128)} %get-tuple-element.307), channel_id=1, source_target_pairs={{0,1},{1,2},{2,3},{4,5},{5,6},{6,7},{8,9},{9,10},{10,11},{12,13},{... | collective-permute-start | bytes 49160 | tf_op jit(solution)/shard_map/ppermute | solution.py:30
  121.9 21.1 %collective-permute-start.25 = (f32[8,1,512]{2,1,0:T(1,128)}, f32[8,1,512]{2,1,0:T(1,128)}, u32[]{:S(2)}, u32[]{:S(2)}) collective-permute-start(f32[8,1,512]{2,1,0:T(1,128)} %get-tuple-element.304), channel_id=1, source_target_pairs={{1,0},{2,1},{3,2},{5,4},{6,5},{7,6},{9,8},{10,9},{11,10},{13,12},{... | collective-permute-start | bytes 49160 | tf_op jit(solution)/shard_map/ppermute | solution.py:30
  123.2 9.3 %collective-permute-start.26 = (f32[8,1,512]{2,1,0:T(1,128)}, f32[8,1,512]{2,1,0:T(1,128)}, u32[]{:S(2)}, u32[]{:S(2)}) collective-permute-start(f32[8,1,512]{2,1,0:T(1,128)} %get-tuple-element.305), channel_id=1, source_target_pairs={{0,4},{4,0},{8,12},{12,8},{1,5},{5,1},{9,13},{13,9},{2,6},{6,2},{1... | collective-permute-start | bytes 49160 | tf_op jit(solution)/shard_map/ppermute | solution.py:18
  132.5 8.7 %collective-permute-start.27 = (f32[8,1,512]{2,1,0:T(1,128)}, f32[8,1,512]{2,1,0:T(1,128)}, u32[]{:S(2)}, u32[]{:S(2)}) collective-permute-start(f32[8,1,512]{2,1,0:T(1,128)} %collective-permute-done.26), channel_id=1, source_target_pairs={{0,8},{8,0},{4,12},{12,4},{1,9},{9,1},{5,13},{13,5},{2,10},{10,2},... | collective-permute-start | bytes 49160 | tf_op jit(solution)/shard_map/ppermute | solution.py:18
  138.0 18.1 %collective-permute-start.32 = (f32[8,32,1]{2,1,0:T(8,128)}, f32[8,32,1]{2,1,0:T(8,128)}, u32[]{:S(2)}, u32[]{:S(2)}) collective-permute-start(f32[8,32,1]{2,1,0:T(8,128)} %slice.655), channel_id=1, source_target_pairs={{0,4},{4,8},{8,12},{12,0},{1,5},{5,9},{9,13},{13,1},{2,6},{6,10},{... | collective-permute-start | bytes 3080 | tf_op jit(solution)/shard_map/ppermute | solution.py:24
  149.9 9.0 %collective-permute-start.38 = (f32[8,1,512]{2,1,0:T(1,128)S(1)}, f32[8,1,512]{2,1,0:T(1,128)S(1)}, u32[]{:S(2)}, u32[]{:S(2)}) collective-permute-start(f32[8,1,512]{2,1,0:T(1,128)S(1)} %get-tuple-element.302), channel_id=1, source_target_pairs={{0,4},{4,0},{8,12},{12,8},{1,5},{5,1},{9,13},{13,9},{2,6},{6,2},{1... | collective-permute-start | bytes 49160 | tf_op jit(solution)/shard_map/ppermute | solution.py:18
  150.0 10.0 %collective-permute-start.34 = (f32[8,1,512]{2,1,0:T(1,128)S(1)}, f32[8,1,512]{2,1,0:T(1,128)S(1)}, u32[]{:S(2)}, u32[]{:S(2)}) collective-permute-start(f32[8,1,512]{2,1,0:T(1,128)S(1)} %get-tuple-element.298), channel_id=1, source_target_pairs={{0,4},{4,0},{8,12},{12,8},{1,5},{5,1},{9,13},{13,9},{2,6},{6,2},{1... | collective-permute-start | bytes 49160 | tf_op jit(solution)/shard_map/ppermute | solution.py:18
  152.1 9.8 %collective-permute-start.33 = (f32[8,1,512]{2,1,0:T(1,128)S(1)}, f32[8,1,512]{2,1,0:T(1,128)S(1)}, u32[]{:S(2)}, u32[]{:S(2)}) collective-permute-start(f32[8,1,512]{2,1,0:T(1,128)S(1)} %get-tuple-element.299), channel_id=1, source_target_pairs={{0,1},{1,2},{2,3},{4,5},{5,6},{6,7},{8,9},{9,10},{10,11},{12,13},{... | collective-permute-start | bytes 49160 | tf_op jit(solution)/shard_map/ppermute | solution.py:30
  156.0 8.3 %collective-permute-start.36 = (f32[8,32,1]{2,1,0:T(8,128)S(1)}, f32[8,32,1]{2,1,0:T(8,128)S(1)}, u32[]{:S(2)}, u32[]{:S(2)}) collective-permute-start(f32[8,32,1]{2,1,0:T(8,128)S(1)} %slice.660), channel_id=1, source_target_pairs={{0,4},{4,8},{8,12},{12,0},{1,5},{5,9},{9,13},{13,1},{2,6},{6,10},{... | collective-permute-start | bytes 3080 | tf_op jit(solution)/shard_map/ppermute | solution.py:24
  156.1 8.2 %collective-permute-start.37 = (f32[8,1,512]{2,1,0:T(1,128)S(1)}, f32[8,1,512]{2,1,0:T(1,128)S(1)}, u32[]{:S(2)}, u32[]{:S(2)}) collective-permute-start(f32[8,1,512]{2,1,0:T(1,128)S(1)} %get-tuple-element.303), channel_id=1, source_target_pairs={{0,1},{1,2},{2,3},{4,5},{5,6},{6,7},{8,9},{9,10},{10,11},{12,13},{... | collective-permute-start | bytes 49160 | tf_op jit(solution)/shard_map/ppermute | solution.py:30
  (44 other events, 243.4 us)
where the time goes:
time: 169 us; the launch traced here: 167 us
  starting transfers between devices  59.1 us (35%)
  local copies, waits for them, and re-layouts  40.2 us (24%)
  other arithmetic  38.5 us (23%)
  waiting for transfers between devices  28 us (17%)
    ppermute x20, starting transfers between devices, partner(): return lax.ppermute(block, axis, route)  22.8 us
    ppermute x10, starting transfers between devices, passed_along(): lax.ppermute(value, axis, [(source, source + steps) for source in range(l...  18.9 us
    ppermute x10, waiting for transfers between devices, shifted(): return lax.ppermute(value, axis, pairs)  17.6 us
    ppermute x10, starting transfers between devices, shifted(): return lax.ppermute(value, axis, pairs)  17.4 us
    rev x10, local copies, waits for them, and re-layouts, mirror_row(): return row[..., ::-1]  11.4 us
    ppermute x20, waiting for transfers between devices, partner(): return lax.ppermute(block, axis, route)  10.4 us
    scatter-add x3, local copies, waits for them, and re-layouts, on_device(): bar_fv.at[..., -1:, :].add(passed_along(bar_south, ('lat', 'sub'), -1))  4.85 us
    scatter-add x3, local copies, waits for them, and re-layouts, on_device(): bar_fv = bar_fv.at[..., -1:, :].add(mirror_row(bar_fold_flux))  4.83 us
  transfers between devices with their start and end apart: 40, of which 11 were waited for; matrix products, arithmetic and copies ran while one was open for 36% of the time, Pallas kernels for 0%

commit v1 on v0

v1 whole, which is shorter than its diff:
```python
import jax
import jax.numpy as jnp
from jax import lax
from jax.experimental import pallas as pl
from jax.experimental.pallas import tpu as pltpu
from jax.sharding import PartitionSpec as P

time_step = 0.5
gravity = 1.0
speed_floor = 0.01

ROWS = ("lat", "sub")
GRID = ("lon", "lat", "sub")
TILE = 8
LANES = 128
DEEP = 4
STATICS = 16
VMEM_LIMIT = 48 * 1024 * 1024


def iota(shape, axis):
    return lax.broadcasted_iota(jnp.int32, shape, axis)


def place():
    row = lax.axis_index("lat") * lax.axis_size("sub") + lax.axis_index("sub")
    last = lax.axis_size("lat") * lax.axis_size("sub") - 1
    return row % 2 == 0, row == last


def kind_of(field, count):
    if field < 3 * count:
        kind = field % 3
        return kind, kind > 0
    static = field - 3 * count
    if static < 12:
        return 1 + (static // 3) % 2, static < 6
    return (0, 1, 2, 0)[static - 12], False


def field_list(adj, rest):
    adj_h, adj_u, adj_v = adj
    traj_u, traj_v, wet_u, wet_v, depth, drag, land = rest
    loads = []
    for sens in range(adj_h.shape[0]):
        for ref in (adj_h, adj_u, adj_v):
            loads.append(lambda ref=ref, sens=sens: ref[sens])
    for ref in (traj_u, traj_v, wet_u, wet_v):
        for step in range(3):
            loads.append(lambda ref=ref, step=step: ref[step].astype(jnp.float32))
    for ref in (depth, drag, drag, land):
        loads.append(lambda ref=ref: ref[...].astype(jnp.float32))
    return loads


def lane_tiles(value):
    return [value[:, at : at + LANES] for at in range(0, value.shape[1], LANES)]


def pack_rows(*refs):
    bottom = field_list(refs[0:3], refs[3:10])
    top = field_list(refs[10:13], refs[13:20])
    one, two = refs[20:22]
    count = refs[0].shape[0]
    even, at_top = place()
    width = refs[0].shape[2]
    lower = iota((TILE, width), 0) < DEEP

    def pair(loads, index, shift_first):
        first, second = loads[index](), loads[index + 1]()
        if shift_first:
            return jnp.where(lower, pltpu.roll(first, DEEP, 0), second)
        return jnp.where(lower, first, pltpu.roll(second, DEEP, 0))

    for tile in range(one.shape[0]):
        from_bottom = pair(bottom, 2 * tile, False)
        from_top = pair(top, 2 * tile, True)
        one[tile] = jnp.where(even, from_top, from_bottom)
        two[tile] = jnp.where(even, from_bottom, from_top)

    @pl.when(at_top)
    def _():
        row = iota((TILE, LANES), 0)
        lane = LANES - 1 - iota((TILE, LANES), 1)
        backward = (2 * TILE - 1 - row) % TILE
        backward_v = (row < 3) * (6 - row) + (row == 3) * 7 + (row > 3) * row
        sign = jnp.where(row == 3, 1.0, -1.0)

        def mirrored(field):
            kind, turned = kind_of(field, count)
            value = top[field]()
            pieces = []
            for piece in lane_tiles(value)[::-1]:
                piece = jnp.take_along_axis(piece, lane, axis=1)
                piece = jnp.take_along_axis(piece, backward_v if kind == 2 else backward, axis=0)
                if turned:
                    piece = piece * sign
                pieces.append(piece)
            return jnp.concatenate(pieces, axis=1)

        for tile in range(one.shape[0]):
            first, second = mirrored(2 * tile), mirrored(2 * tile + 1)
            two[tile] = jnp.where(lower, first, pltpu.roll(second, DEEP, 0))


def group_lanes(field):
    return field // 32, DEEP * (field % 32)


def pack_columns_own(*refs):
    west = field_list(refs[0:3], refs[3:10])
    east = field_list(refs[10:13], refs[13:20])
    to_west, to_east = refs[20:22]
    rows = refs[0].shape[1]
    lane = iota((rows, LANES), 1)
    for loads, target, origin in ((west, to_west, 0), (east, to_east, LANES - DEEP)):
        packed = [None, None]
        for field, load in enumerate(loads):
            side, at = group_lanes(field)
            value = load()
            shift = (at - origin) % LANES
            if shift:
                value = pltpu.roll(value, shift, 1)
            packed[side] = value if packed[side] is None else jnp.where(lane >= at, value, packed[side])
        for side in range(2):
            target[:, side * LANES : (side + 1) * LANES] = packed[side]


def merge_rows(one, two, own_west, own_east, halo, halo_static, to_west, to_east):
    even, _ = place()
    width = one.shape[2]
    rows = own_west.shape[0]
    lower = iota((TILE, width), 0) < DEEP
    lane = iota((TILE, LANES), 1)
    to_west[:rows, :] = own_west[...]
    to_east[:rows, :] = own_east[...]
    packed = [[None, None], [None, None]]
    for tile in range(one.shape[0]):
        north = jnp.where(even, one[tile], two[tile])
        south = jnp.where(even, two[tile], one[tile])
        first = jnp.where(lower, north, pltpu.roll(south, DEEP, 0))
        second = jnp.where(lower, pltpu.roll(north, DEEP, 0), south)
        for field, value in ((2 * tile, first), (2 * tile + 1, second)):
            if field < halo.shape[0]:
                halo[field] = value
            else:
                halo_static[field - halo.shape[0]] = value
            side, at = group_lanes(field)
            pieces = lane_tiles(value)
            for way, piece, origin in ((0, pieces[0], 0), (1, pieces[-1], LANES - DEEP)):
                shift = (at - origin) % LANES
                if shift:
                    piece = pltpu.roll(piece, shift, 1)
                held = packed[way][side]
                packed[way][side] = piece if held is None else jnp.where(lane >= at, piece, held)
    for way, target in ((0, to_west), (1, to_east)):
        for side in range(2):
            target[rows:, side * LANES : (side + 1) * LANES] = packed[way][side]


def steps_kernel(
    adj_h, adj_u, adj_v, traj_u, traj_v, wet_u, wet_v, depth, drag, land,
    halo, halo_static, from_west, from_east,
    out_h, out_u, out_v, out_depth, out_drag,
    mask_u_s, mask_v_s, keep_u_s, keep_v_s, drag_u_s, drag_v_s, vel_u_s, vel_v_s,
    depth_u_s, depth_v_s, ratio_u_s, ratio_v_s, land_s,
):
    _, at_top = place()
    rows, width = adj_h.shape[1:]
    count = rows // TILE + 1
    last = count - 1
    wide = width + LANES
    row = iota((TILE, wide), 0)
    lane = iota((TILE, LANES), 1)
    sens = pl.program_id(0)

    def corner(field_side, at, tile):
        here = slice(tile * TILE, (tile + 1) * TILE)
        cols = slice(field_side * LANES, (field_side + 1) * LANES)
        east = pltpu.roll(from_east[here, cols], (LANES - at) % LANES, 1)
        west = pltpu.roll(from_west[here, cols], (2 * LANES - DEEP - at) % LANES, 1)
        return jnp.where(lane < LANES // 2, east, west)

    def extended(own, halo_rows, side, at, kind):
        out = []
        for tile in range(count):
            body = own(tile) if tile < last else halo_rows()
            value = jnp.concatenate([body, corner(side, at, tile)], axis=1)
            if tile == last and kind == 1:
                value = jnp.where(at_top & (row < DEEP), pltpu.roll(value, wide - 1, 1), value)
            out.append(value)
        return out

    def east_of(value):
        return pltpu.roll(value, wide - 1, 1)

    def west_of(value):
        return pltpu.roll(value, 1, 1)

    def south_of(values, tile):
        return jnp.where(row == 0, pltpu.roll(values[tile - 1], 1, 0), pltpu.roll(values[tile], 1, 0))

    def north_of(values, tile):
        return jnp.where(
            row == TILE - 1,
            pltpu.roll(values[(tile + 1) % count], TILE - 1, 0),
            pltpu.roll(values[tile], TILE - 1, 0),
        )

    def rows_of(tile):
        return slice(tile * TILE, (tile + 1) * TILE)

    @pl.when(sens == 0)
    def _():
        first_static = 3 * adj_count

        def static(index, ref):
            side, at = group_lanes(first_static + index)
            kind, _ = kind_of(first_static + index, adj_count)
            return extended(
                lambda tile: ref[rows_of(tile), :].astype(jnp.float32),
                lambda: halo_static[index],
                side,
                at,
                kind,
            )

        cells = [jnp.where(value > 0.0, value, 1.0) for value in static(12, depth)]
        drag_u = static(13, drag)
        drag_v = static(14, drag)
        sea = static(15, land)
        face_u = [0.5 * (value + east_of(value)) for value in cells]
        face_v = [0.5 * (cells[tile] + north_of(cells, tile)) for tile in range(count)]
        face_v[last] = jnp.where(row == 3, pltpu.roll(face_v[last - 1], DEEP, 0), face_v[last])
        for tile in range(count):
            here = rows_of(tile)
            land_s[here, :] = 0.5 * sea[tile]
            inverse_u = 1.0 / face_u[tile]
            inverse_v = 1.0 / face_v[tile]
            depth_u_s[here, :] = face_u[tile]
            depth_v_s[here, :] = face_v[tile]
            ratio_u_s[here, :] = -drag_u[tile] * inverse_u
            ratio_v_s[here, :] = -drag_v[tile] * inverse_v
        for step in range(3):
            for vel_index, wet_index, vel_ref, wet_ref, depth_s, ratio_s, mask_s, keep_s, drag_s, vel_s in (
                (step, 6 + step, traj_u, wet_u, depth_u_s, ratio_u_s, mask_u_s, keep_u_s, drag_u_s, vel_u_s),
                (3 + step, 9 + step, traj_v, wet_v, depth_v_s, ratio_v_s, mask_v_s, keep_v_s, drag_v_s, vel_v_s),
            ):
                vel = static(vel_index, vel_ref.at[step])
                wet = static(wet_index, wet_ref.at[step])
                for tile in range(count):
                    here = rows_of(tile)
                    square = vel[tile] * vel[tile]
                    speed = jnp.sqrt(square + speed_floor)
                    mask_s[step, here, :] = 0.5 * wet[tile]
                    keep_s[step, here, :] = 2.0 + ratio_s[here, :] * (speed + square / speed)
                    drag_s[step, here, :] = -vel[tile] * speed / depth_s[here, :]
                    vel_s[step, here, :] = vel[tile]

    def dynamic(kind, ref):
        return extended(
            lambda tile: ref[0, rows_of(tile), :],
            lambda: halo[kind],
            0,
            DEEP * (3 * sens + kind),
            kind,
        )

    bar_h, bar_u, bar_v = dynamic(0, adj_h), dynamic(1, adj_u), dynamic(2, adj_v)
    sum_xu, sum_xv, sum_u, sum_v = ([None] * count for _ in range(4))

    def add_to(sums, tile, value):
        sums[tile] = value if sums[tile] is None else sums[tile] + value

    for step in (2, 1, 0):
        flow_u, flow_v, flow_v_face, sea = [], [], [], []
        for tile in range(count):
            here = rows_of(tile)
            flow_u.append(mask_u_s[step, here, :] * bar_u[tile])
            flow_v.append(mask_v_s[step, here, :] * bar_v[tile])
        flow_v_face = list(flow_v)
        flow_v_face[last - 1] = flow_v[last - 1] - jnp.where(
            at_top & (row == TILE - 1), pltpu.roll(flow_v[last], DEEP, 0), 0.0
        )
        for tile in range(count):
            here = rows_of(tile)
            bar_h[tile] = (
                bar_h[tile]
                + (flow_u[tile] - west_of(flow_u[tile]))
                + (flow_v_face[tile] - south_of(flow_v_face, tile))
            )
            sea.append(land_s[here, :] * bar_h[tile])
        for tile in range(count):
            here = rows_of(tile)
            turn_u = east_of(sea[tile]) - sea[tile]
            turn_v = north_of(sea, tile) - sea[tile]
            if tile == last:
                turn_v = jnp.where(row == 3, -pltpu.roll(fold_turn, DEEP, 0), turn_v)
            fold_turn = turn_v
            bar_u[tile] = keep_u_s[step, here, :] * flow_u[tile] + depth_u_s[here, :] * turn_u
            bar_v[tile] = keep_v_s[step, here, :] * flow_v[tile] + depth_v_s[here, :] * turn_v
            add_to(sum_xu, tile, drag_u_s[step, here, :] * flow_u[tile])
            add_to(sum_xv, tile, drag_v_s[step, here, :] * flow_v[tile])
            add_to(sum_u, tile, vel_u_s[step, here, :] * turn_u)
            add_to(sum_v, tile, vel_v_s[step, here, :] * turn_v)

    face_v = [
        ratio_v_s[rows_of(tile), :] * sum_xv[tile] + sum_v[tile] for tile in range(count)
    ]
    for tile in range(last):
        here = rows_of(tile)
        face_u = ratio_u_s[here, :] * sum_xu[tile] + sum_u[tile]
        total = face_u + west_of(face_u) + face_v[tile] + south_of(face_v, tile)
        if tile == last - 1:
            total = total + jnp.where(
                at_top & (row == TILE - 1), pltpu.roll(face_v[last], DEEP, 0), 0.0
            )
        out_h[0, here, :] = bar_h[tile][:, :width]
        out_u[0, here, :] = bar_u[tile][:, :width]
        out_v[0, here, :] = bar_v[tile][:, :width]
        out_depth[0, here, :] = 0.5 * total[:, :width]
        out_drag[0, here, :] = (sum_xu[tile] + sum_xv[tile])[:, :width]


adj_count = 8


def on_device(traj_u, traj_v, adj_h, adj_u, adj_v, depth, drag, land, wet_u, wet_v):
    count, rows, width = adj_h.shape
    steps = traj_u.shape[0]
    fields = 3 * count + STATICS
    args = (adj_h, adj_u, adj_v, traj_u, traj_v, wet_u, wet_v, depth, drag, land)

    def blocks(shape, where):
        specs = []
        for arg in args:
            specs.append(pl.BlockSpec(arg.shape[:-2] + shape, (lambda n: lambda *_: (0,) * n + where)(arg.ndim - 2)))
        return specs

    params = pltpu.CompilerParams(vmem_limit_bytes=VMEM_LIMIT)
    row_pack = jax.ShapeDtypeStruct((fields // 2, TILE, width), jnp.float32)
    one, two = pl.pallas_call(
        pack_rows,
        grid=(1,),
        in_specs=blocks((TILE, width), (0, 0)) + blocks((TILE, width), (rows // TILE - 1, 0)),
        out_specs=[pl.BlockSpec(row_pack.shape, lambda *_: (0, 0, 0))] * 2,
        out_shape=[row_pack] * 2,
        compiler_params=params,
        name="pack_rows",
    )(*args, *args)

    lons, lats, subs = (lax.axis_size(axis) for axis in GRID)
    total_rows = lats * subs

    def device(lon, row):
        return lon * total_rows + row

    one = lax.ppermute(one, "sub", [(core, core ^ 1) for core in range(subs)])
    route = []
    for lon in range(lons):
        for row in range(1, total_rows - 1, 2):
            route += [(device(lon, row), device(lon, row + 1)), (device(lon, row + 1), device(lon, row))]
        route.append((device(lon, total_rows - 1), device(lons - 1 - lon, total_rows - 1)))
    two = lax.ppermute(two, GRID, route)

    own_pack = jax.ShapeDtypeStruct((rows, 2 * LANES), jnp.float32)
    own_west, own_east = pl.pallas_call(
        pack_columns_own,
        grid=(1,),
        in_specs=blocks((rows, LANES), (0, 0)) + blocks((rows, LANES), (0, width // LANES - 1)),
        out_specs=[pl.BlockSpec(own_pack.shape, lambda *_: (0, 0))] * 2,
        out_shape=[own_pack] * 2,
        compiler_params=params,
        name="pack_columns",
    )(*args, *args)

    full_pack = jax.ShapeDtypeStruct((rows + TILE, 2 * LANES), jnp.float32)
    halo, halo_static, to_west, to_east = pl.pallas_call(
        merge_rows,
        out_shape=[
            jax.ShapeDtypeStruct((3 * count, TILE, width), jnp.float32),
            jax.ShapeDtypeStruct((STATICS, TILE, width), jnp.float32),
            full_pack,
            full_pack,
        ],
        compiler_params=params,
        name="merge_rows",
    )(one, two, own_west, own_east)
    from_east = lax.ppermute(to_west, "lon", [(lon, (lon - 1) % lons) for lon in range(lons)])
    from_west = lax.ppermute(to_east, "lon", [(lon, (lon + 1) % lons) for lon in range(lons)])

    def whole(shape):
        return pl.BlockSpec(shape, lambda sens: (0,) * len(shape))

    block = pl.BlockSpec((1, rows, width), lambda sens: (sens, 0, 0))
    out = jax.ShapeDtypeStruct(adj_h.shape, jnp.float32)
    ext = (rows + TILE, width + LANES)
    return pl.pallas_call(
        steps_kernel,
        grid=(count,),
        in_specs=[block] * 3
        + [whole(arg.shape) for arg in args[3:]]
        + [
            pl.BlockSpec((3, TILE, width), lambda sens: (sens, 0, 0)),
            pl.BlockSpec((STATICS, TILE, width), lambda sens: (0, 0, 0)),
            whole(full_pack.shape),
            whole(full_pack.shape),
        ],
        out_specs=[block] * 5,
        out_shape=[out] * 5,
        scratch_shapes=[pltpu.VMEM((steps,) + ext, jnp.float32)] * 8 + [pltpu.VMEM(ext, jnp.float32)] * 5,
        compiler_params=params,
        name="reverse_steps",
    )(*args, halo, halo_static, from_west, from_east)


def solution(mesh):
    state = P("case", ROWS, "lon")
    fixed = P(ROWS, "lon")
    return jax.shard_map(
        on_device,
        mesh=mesh,
        in_specs=(state,) * 5 + (fixed,) * 3 + (state,) * 2,
        out_specs=(state,) * 5,
        check_vma=False,
    )
```

time: 169 us -> 33.8 us (0.20)
  the two profiles are of different devices: /device:TPU:0 before, /device:TPU:3 now
where the time goes in v1:
time: 33.8 us; the launch traced here: 33.3 us
  local copies, waits for them, and re-layouts  9.36 us (28%)
  starting transfers between devices  9.09 us (27%)
  Pallas kernels  7.64 us (23%)
  waiting for transfers between devices  6.46 us (19%)
  between operations  0.72 us (2%)
    unnamed x26, local copies, waits for them, and re-layouts  9.36 us
    pallas_call x1, Pallas kernels, on_device(): pl.pallas_call(steps_kernel, grid=(count,), in_specs=[block] * 3 + [whole...  6.73 us
    ppermute x1, starting transfers between devices, on_device(): two = lax.ppermute(two, GRID, route)  5.22 us
    ppermute x1, waiting for transfers between devices, on_device(): two = lax.ppermute(two, GRID, route)  4.09 us
    ppermute x1, starting transfers between devices, on_device(): lax.ppermute(to_east, 'lon', [(lon, (lon + 1) % lons) for lon in range(lo...  2.89 us
    ppermute x1, waiting for transfers between devices, on_device(): lax.ppermute(to_east, 'lon', [(lon, (lon + 1) % lons) for lon in range(lo...  1.44 us
    ppermute x1, waiting for transfers between devices, on_device(): lax.ppermute(to_west, 'lon', [(lon, (lon - 1) % lons) for lon in range(lo...  0.93 us
  transfers between devices with their start and end apart: 4, of which 3 were waited for; matrix products, arithmetic and copies ran while one was open for 0% of the time, Pallas kernels for 1%

profile of v1, /device:TPU:3, one launch (start us, length us, event | category | flops | bytes accessed | tf_op | source)
XLA Modules:
  0.0 33.3 jit_solution(12041713354317929335)
XLA Ops:
  0.6 0.0 copy-start
  0.6 1.0 %copy-done = f32[8,32,512]{2,1,0:T(8,128)S(1)} copy-done((f32[8,32,512]{2,1,0:T(8,128)S(1)}, f32[8,32,512]{2,1,0:T(8,128)}, u32[]{:S(2)}) %copy-start) | copy-done | bytes 524312
  1.7 1.0 %copy-done.2 = f32[8,32,512]{2,1,0:T(8,128)S(1)} copy-done((f32[8,32,512]{2,1,0:T(8,128)S(1)}, f32[8,32,512]{2,1,0:T(8,128)}, u32[]{:S(2)}) %copy-start.2) | copy-done | bytes 524312
  2.7 1.0 %copy-done.4 = f32[8,32,512]{2,1,0:T(8,128)S(1)} copy-done((f32[8,32,512]{2,1,0:T(8,128)S(1)}, f32[8,32,512]{2,1,0:T(8,128)}, u32[]{:S(2)}) %copy-start.4) | copy-done | bytes 524312
  3.8 0.9 %copy-done.6 = f32[3,32,512]{2,1,0:T(8,128)S(1)} copy-done((f32[3,32,512]{2,1,0:T(8,128)S(1)}, f32[3,32,512]{2,1,0:T(8,128)}, u32[]{:S(2)}) %copy-start.6) | copy-done | bytes 196632
  4.7 0.9 %copy-done.7 = f32[3,32,512]{2,1,0:T(8,128)S(1)} copy-done((f32[3,32,512]{2,1,0:T(8,128)S(1)}, f32[3,32,512]{2,1,0:T(8,128)}, u32[]{:S(2)}) %copy-start.7) | copy-done | bytes 196632
  5.6 0.9 %copy-done.8 = s32[3,32,512]{2,1,0:T(8,128)S(1)} copy-done((s32[3,32,512]{2,1,0:T(8,128)S(1)}, s32[3,32,512]{2,1,0:T(8,128)}, u32[]{:S(2)}) %copy-start.8) | copy-done | bytes 196632
  6.5 0.9 %copy-done.9 = s32[3,32,512]{2,1,0:T(8,128)S(1)} copy-done((s32[3,32,512]{2,1,0:T(8,128)S(1)}, s32[3,32,512]{2,1,0:T(8,128)}, u32[]{:S(2)}) %copy-start.9) | copy-done | bytes 196632
  7.5 0.8 %copy-done.10 = f32[32,512]{1,0:T(8,128)S(1)} copy-done((f32[32,512]{1,0:T(8,128)S(1)}, f32[32,512]{1,0:T(8,128)}, u32[]{:S(2)}) %copy-start.10) | copy-done | bytes 65560
  8.3 0.8 %copy-done.11 = f32[32,512]{1,0:T(8,128)S(1)} copy-done((f32[32,512]{1,0:T(8,128)S(1)}, f32[32,512]{1,0:T(8,128)}, u32[]{:S(2)}) %copy-start.11) | copy-done | bytes 65560
  9.2 0.8 %copy-done.12 = s32[32,512]{1,0:T(8,128)S(1)} copy-done((s32[32,512]{1,0:T(8,128)S(1)}, s32[32,512]{1,0:T(8,128)}, u32[]{:S(2)}) %copy-start.12) | copy-done | bytes 65560
  10.0 0.3 %pack_rows.1 = (f32[20,8,512]{2,1,0:T(8,128)S(1)}, f32[20,8,512]{2,1,0:T(8,128)S(1)}) custom-call(f32[8,32,512]{2,1,0:T(8,128)S(1)} %copy-done, f32[8,32,512]{2,1,0:T(8,128)S(1)} %copy-done.2, f32[8,32,512]{2,1,0:T(8,128)S(1)} %copy-done.4, f32[3,32,512]{2,1,0:T(8,128)S(1)} %copy-done.6, f32[3,32,512]{2,1,0:T(8,128)S(1)} %copy-done.7, ...), custom_call_target="tpu_custom_call" | custom-call | tf_op jit(solution)/shard_map/pack_rows/pallas_call | solution.py:342
  10.3 0.5 %collective-permute-start = (f32[20,8,512]{2,1,0:T(8,128)S(1)}, f32[20,8,512]{2,1,0:T(8,128)S(1)}, u32[]{:S(2)}, u32[]{:S(2)}) collective-permute-start(f32[20,8,512]{2,1,0:T(8,128)S(1)} %get-tuple-element.13), channel_id=1, source_target_pairs={{0,1},{1,0},{2,3},{3,2},{4,5},{5,4},{6,7},{7,6},{8,9},{9,8},{10,11... | collective-permute-start | bytes 983048 | tf_op jit(solution)/shard_map/ppermute | solution.py:358
  10.9 5.2 %collective-permute-start.1 = (f32[20,8,512]{2,1,0:T(8,128)S(1)}, f32[20,8,512]{2,1,0:T(8,128)S(1)}, u32[]{:S(2)}, u32[]{:S(2)}) collective-permute-start(f32[20,8,512]{2,1,0:T(8,128)S(1)} %get-tuple-element.14), channel_id=1, source_target_pairs={{1,2},{2,1},{3,15},{5,6},{6,5},{7,11},{9,10},{10,9},{11,7},{13,14}... | collective-permute-start | bytes 983048 | tf_op jit(solution)/shard_map/ppermute | solution.py:364
  16.1 0.0 copy-start.3
  16.1 0.0 copy-start.5
  16.1 0.4 %pack_columns.1 = (f32[32,256]{1,0:T(8,128)S(1)}, f32[32,256]{1,0:T(8,128)S(1)}) custom-call(f32[8,32,512]{2,1,0:T(8,128)S(1)} %copy-done, f32[8,32,512]{2,1,0:T(8,128)S(1)} %copy-done.2, f32[8,32,512]{2,1,0:T(8,128)S(1)} %copy-done.4, f32[3,32,512]{2,1,0:T(8,128)S(1)} %copy-done.6, f32[3,32,512]{2,1,0:T(8,128)S(1)} %copy-done.7, ...), custom_call_target="tpu_custom_call" | custom-call | tf_op jit(solution)/shard_map/pack_columns/pallas_call | solution.py:367
  16.5 4.1 %collective-permute-done.1.two = f32[20,8,512]{2,1,0:T(8,128)S(1)} collective-permute-done((f32[20,8,512]{2,1,0:T(8,128)S(1)}, f32[20,8,512]{2,1,0:T(8,128)S(1)}, u32[]{:S(2)}, u32[]{:S(2)}) %collective-permute-start.1) | collective-permute-done | bytes 327712 | tf_op jit(solution)/shard_map/ppermute | solution.py:364
  20.6 0.2 merge_rows.1
  20.8 2.9 %collective-permute-start.2 = (f32[40,256]{1,0:T(8,128)S(1)}, f32[40,256]{1,0:T(8,128)S(1)}, u32[]{:S(2)}, u32[]{:S(2)}) collective-permute-start(f32[40,256]{1,0:T(8,128)S(1)} %get-tuple-element.19), channel_id=1, source_target_pairs={{0,4},{4,8},{8,12},{12,0},{1,5},{5,9},{9,13},{13,1},{2,6},{6,10},{... | collective-permute-start | bytes 122888 | tf_op jit(solution)/shard_map/ppermute | solution.py:390
  23.7 0.5 %collective-permute-start.3 = (f32[40,256]{1,0:T(8,128)S(1)}, f32[40,256]{1,0:T(8,128)S(1)}, u32[]{:S(2)}, u32[]{:S(2)}) collective-permute-start(f32[40,256]{1,0:T(8,128)S(1)} %get-tuple-element.20), channel_id=1, source_target_pairs={{0,12},{4,0},{8,4},{12,8},{1,13},{5,1},{9,5},{13,9},{2,14},{6,2},{... | collective-permute-start | bytes 122888 | tf_op jit(solution)/shard_map/ppermute | solution.py:389
  24.2 1.4 %collective-permute-done.2.from_west = f32[40,256]{1,0:T(8,128)S(1)} collective-permute-done((f32[40,256]{1,0:T(8,128)S(1)}, f32[40,256]{1,0:T(8,128)S(1)}, u32[]{:S(2)}, u32[]{:S(2)}) %collective-permute-start.2) | collective-permute-done | bytes 40992 | tf_op jit(solution)/shard_map/ppermute | solution.py:390
  25.6 0.9 %collective-permute-done.3.from_east = f32[40,256]{1,0:T(8,128)S(1)} collective-permute-done((f32[40,256]{1,0:T(8,128)S(1)}, f32[40,256]{1,0:T(8,128)S(1)}, u32[]{:S(2)}, u32[]{:S(2)}) %collective-permute-start.3) | collective-permute-done | bytes 40992 | tf_op jit(solution)/shard_map/ppermute | solution.py:389
  26.5 6.7 %reverse_steps.1 = (f32[8,32,512]{2,1,0:T(8,128)}, f32[8,32,512]{2,1,0:T(8,128)}, f32[8,32,512]{2,1,0:T(8,128)}, f32[8,32,512]{2,1,0:T(8,128)}, f32[8,32,512]{2,1,0:T(8,128)}) custom-call(f32[8,32,512]{2,1,0:T(8,128)S(1)} %copy-done.1, f32[8,32,512]{2,1,0:T(8,128)S(1)} %copy-done.3, f32[8,32,512]{2,1,0:T(8,128)S(1)} %copy-done.5, ...), custom_call_target="tpu_custom_call" | custom-call | tf_op jit(solution)/shard_map/reverse_steps/pallas_call | solution.py:398
  (14 shorter events, 0.0 us)
Async XLA Ops:
  0.6 1.0 %copy-start = (f32[8,32,512]{2,1,0:T(8,128)S(1)}, f32[8,32,512]{2,1,0:T(8,128)}, u32[]{:S(2)}) copy-start(f32[8,32,512]{2,1,0:T(8,128)} %adj_h.1) | copy-start | bytes 1572868
  1.7 1.0 %copy-start.2 = (f32[8,32,512]{2,1,0:T(8,128)S(1)}, f32[8,32,512]{2,1,0:T(8,128)}, u32[]{:S(2)}) copy-start(f32[8,32,512]{2,1,0:T(8,128)} %adj_u.1) | copy-start | bytes 1572868
  2.7 1.0 %copy-start.4 = (f32[8,32,512]{2,1,0:T(8,128)S(1)}, f32[8,32,512]{2,1,0:T(8,128)}, u32[]{:S(2)}) copy-start(f32[8,32,512]{2,1,0:T(8,128)} %adj_v.1) | copy-start | bytes 1572868
  3.8 0.9 %copy-start.6 = (f32[3,32,512]{2,1,0:T(8,128)S(1)}, f32[3,32,512]{2,1,0:T(8,128)}, u32[]{:S(2)}) copy-start(f32[3,32,512]{2,1,0:T(8,128)} %traj_u.1) | copy-start | bytes 589828
  4.7 0.9 %copy-start.7 = (f32[3,32,512]{2,1,0:T(8,128)S(1)}, f32[3,32,512]{2,1,0:T(8,128)}, u32[]{:S(2)}) copy-start(f32[3,32,512]{2,1,0:T(8,128)} %traj_v.1) | copy-start | bytes 589828
  5.6 0.9 %copy-start.8 = (s32[3,32,512]{2,1,0:T(8,128)S(1)}, s32[3,32,512]{2,1,0:T(8,128)}, u32[]{:S(2)}) copy-start(s32[3,32,512]{2,1,0:T(8,128)} %wet_u.1) | copy-start | bytes 589828
  6.5 0.9 %copy-start.9 = (s32[3,32,512]{2,1,0:T(8,128)S(1)}, s32[3,32,512]{2,1,0:T(8,128)}, u32[]{:S(2)}) copy-start(s32[3,32,512]{2,1,0:T(8,128)} %wet_v.1) | copy-start | bytes 589828
  7.5 0.8 %copy-start.10 = (f32[32,512]{1,0:T(8,128)S(1)}, f32[32,512]{1,0:T(8,128)}, u32[]{:S(2)}) copy-start(f32[32,512]{1,0:T(8,128)} %depth.1) | copy-start | bytes 196612
  8.3 0.8 %copy-start.11 = (f32[32,512]{1,0:T(8,128)S(1)}, f32[32,512]{1,0:T(8,128)}, u32[]{:S(2)}) copy-start(f32[32,512]{1,0:T(8,128)} %drag.1) | copy-start | bytes 196612
  9.2 0.8 %copy-start.12 = (s32[32,512]{1,0:T(8,128)S(1)}, s32[32,512]{1,0:T(8,128)}, u32[]{:S(2)}) copy-start(s32[32,512]{1,0:T(8,128)} %land.1) | copy-start | bytes 196612
  10.3 6.2 %collective-permute-start = (f32[20,8,512]{2,1,0:T(8,128)S(1)}, f32[20,8,512]{2,1,0:T(8,128)S(1)}, u32[]{:S(2)}, u32[]{:S(2)}) collective-permute-start(f32[20,8,512]{2,1,0:T(8,128)S(1)} %get-tuple-element.13), channel_id=1, source_target_pairs={{0,1},{1,0},{2,3},{3,2},{4,5},{5,4},{6,7},{7,6},{8,9},{9,8},{10,11... | collective-permute-start | bytes 983048 | tf_op jit(solution)/shard_map/ppermute | solution.py:358
  10.9 9.8 %collective-permute-start.1 = (f32[20,8,512]{2,1,0:T(8,128)S(1)}, f32[20,8,512]{2,1,0:T(8,128)S(1)}, u32[]{:S(2)}, u32[]{:S(2)}) collective-permute-start(f32[20,8,512]{2,1,0:T(8,128)S(1)} %get-tuple-element.14), channel_id=1, source_target_pairs={{1,2},{2,1},{3,15},{5,6},{6,5},{7,11},{9,10},{10,9},{11,7},{13,14}... | collective-permute-start | bytes 983048 | tf_op jit(solution)/shard_map/ppermute | solution.py:364
  16.1 10.5 %copy-start.3 = (f32[8,32,512]{2,1,0:T(8,128)S(1)}, f32[8,32,512]{2,1,0:T(8,128)}, u32[]{:S(2)}) copy-start(f32[8,32,512]{2,1,0:T(8,128)} %adj_u.1) | copy-start | bytes 1572868
  16.1 10.4 %copy-start.5 = (f32[8,32,512]{2,1,0:T(8,128)S(1)}, f32[8,32,512]{2,1,0:T(8,128)}, u32[]{:S(2)}) copy-start(f32[8,32,512]{2,1,0:T(8,128)} %adj_v.1) | copy-start | bytes 1572868
  16.5 10.0 %copy-start.1 = (f32[8,32,512]{2,1,0:T(8,128)S(1)}, f32[8,32,512]{2,1,0:T(8,128)}, u32[]{:S(2)}) copy-start(f32[8,32,512]{2,1,0:T(8,128)} %adj_h.1) | copy-start | bytes 1572868
  20.8 4.8 %collective-permute-start.2 = (f32[40,256]{1,0:T(8,128)S(1)}, f32[40,256]{1,0:T(8,128)S(1)}, u32[]{:S(2)}, u32[]{:S(2)}) collective-permute-start(f32[40,256]{1,0:T(8,128)S(1)} %get-tuple-element.19), channel_id=1, source_target_pairs={{0,4},{4,8},{8,12},{12,0},{1,5},{5,9},{9,13},{13,1},{2,6},{6,10},{... | collective-permute-start | bytes 122888 | tf_op jit(solution)/shard_map/ppermute | solution.py:390
  23.7 2.9 %collective-permute-start.3 = (f32[40,256]{1,0:T(8,128)S(1)}, f32[40,256]{1,0:T(8,128)S(1)}, u32[]{:S(2)}, u32[]{:S(2)}) collective-permute-start(f32[40,256]{1,0:T(8,128)S(1)} %get-tuple-element.20), channel_id=1, source_target_pairs={{0,12},{4,0},{8,4},{12,8},{1,13},{5,1},{9,5},{13,9},{2,14},{6,2},{... | collective-permute-start | bytes 122888 | tf_op jit(solution)/shard_map/ppermute | solution.py:389

commit v2 on v1

v2 whole, which is shorter than its diff:
```python
import functools

import jax
import jax.numpy as jnp
from jax import lax
from jax.experimental import pallas as pl
from jax.experimental.pallas import tpu as pltpu
from jax.sharding import PartitionSpec as P

time_step = 0.5
gravity = 1.0
speed_floor = 0.01

ROWS = ("lat", "sub")
GRID = ("lon", "lat", "sub")
TILE = 8
LANES = 128
DEEP = 4
VMEM_LIMIT = 48 * 1024 * 1024


def iota(shape, axis):
    return lax.broadcasted_iota(jnp.int32, shape, axis)


def place():
    row = lax.axis_index("lat") * lax.axis_size("sub") + lax.axis_index("sub")
    last = lax.axis_size("lat") * lax.axis_size("sub") - 1
    return row % 2 == 0, row == last


STATE_SLOTS = (3, 3, 4)
SHARED = (
    (("traj_v", 2), 2, 3, True),
    (("traj_v", 1), 2, 2, True),
    (("traj_v", 0), 2, 1, True),
    (("traj_u", 2), 1, 2, True),
    (("traj_u", 1), 1, 1, True),
    (("wet_v", 1), 2, 3, False),
    (("wet_v", 0), 2, 2, False),
    (("wet_u", 1), 1, 2, False),
    (("wet_u", 0), 1, 1, False),
    (("depth", None), 0, 3, False),
    (("drag", None), 3, 3, False),
    (("land", None), 0, 3, False),
)
NAMES = ("adj_h", "adj_u", "adj_v", "traj_u", "traj_v", "wet_u", "wet_v", "depth", "drag", "land")
TILES = tuple(entry[0] for entry in SHARED[:10]) + (("drag", 1), ("drag", 2), ("land", None), ("traj_u", 0))


def load(refs, name, step):
    value = refs[name][...] if step is None or name == "drag" else refs[name][step]
    return value.astype(jnp.float32)


def message_rows(count):
    rows = sum(STATE_SLOTS) * count + sum(entry[2] for entry in SHARED)
    return -(-rows // TILE) * TILE


def row_plan(count):
    plan, at = [], 0
    for sens in range(count):
        for kind in range(3):
            plan.append(((NAMES[kind], sens), kind, kind > 0, at, STATE_SLOTS[kind]))
            at += STATE_SLOTS[kind]
    for key, kind, slots, turned in SHARED:
        plan.append((key, kind, turned, at, slots))
        at += slots
    return plan


def lane_tiles(value):
    return [value[:, at : at + LANES] for at in range(0, value.shape[1], LANES)]


def masked(refs, key):
    name, step = key
    value = load(refs, name, step)
    if name == "adj_u":
        value = value * load(refs, "wet_u", 2)
    if name == "adj_v":
        value = value * load(refs, "wet_v", 2)
    return value


def pack_rows(*refs):
    arrays = dict(zip(NAMES, refs[:10]))
    one, two = refs[10:12]
    bottom = dict(zip(NAMES, refs[12:22]))
    top = dict(zip(NAMES, refs[22:32]))
    sems = refs[32]
    count, rows, width = arrays["adj_h"].shape
    even, at_top = place()
    copies = {}
    order = ("wet_u", "wet_v", "adj_h", "adj_u", "adj_v", "traj_u", "traj_v", "depth", "drag", "land")
    for number, name in enumerate(order):
        array = arrays[name]
        lead = (slice(None),) * (array.ndim - 2)
        pair = []
        for side, (held, first) in enumerate(((bottom, 0), (top, rows - TILE))):
            pair.append(
                pltpu.make_async_copy(array.at[lead + (pl.ds(first, TILE),)], held[name], sems.at[number, side])
            )
        for copy in pair:
            copy.start()
        copies[name] = pair
    for name in order:
        for copy in copies[name]:
            copy.wait()

    plan = row_plan(count)
    for key, kind, turned, at, slots in plan:
        low = masked(bottom, key)[:slots]
        high = masked(top, key)[TILE - slots :]
        here = slice(at, at + slots)
        one[here, :] = jnp.where(even, high, low)
        two[here, :] = jnp.where(even, low, high)

    @pl.when(at_top)
    def _():
        row = iota((TILE, LANES), 0)
        lane = LANES - 1 - iota((TILE, LANES), 1)
        for key, kind, turned, at, slots in plan:
            value = masked(top, key)
            sources = [TILE - 1 - slot for slot in range(slots)]
            if kind == 2:
                sources = [TILE - 2 - slot for slot in range(slots - 1)] + [TILE - 1]
            order = jnp.zeros((TILE, LANES), jnp.int32)
            for slot, source in enumerate(sources):
                order = jnp.where(row == slot, source, order)
            pieces = []
            for piece in lane_tiles(value)[::-1]:
                piece = jnp.take_along_axis(piece, lane, axis=1)
                piece = jnp.take_along_axis(piece, order, axis=0)
                if turned:
                    piece = jnp.where(row == slots - 1, piece, -piece) if kind == 2 else -piece
                pieces.append(piece)
            two[at : at + slots, :] = jnp.concatenate(pieces, axis=1)[:slots]


def group_lanes(field):
    return field // 32, DEEP * (field % 32)


def column_fields(count):
    return [(NAMES[kind], sens) for sens in range(count) for kind in range(3)] + list(TILES)


def pack_columns_own(*refs):
    arrays = dict(zip(NAMES, refs[:10]))
    to_west, to_east = refs[10:12]
    west = dict(zip(NAMES, refs[12:22]))
    east = dict(zip(NAMES, refs[22:32]))
    sems = refs[32]
    count, rows, width = arrays["adj_h"].shape
    copies = []
    for number, name in enumerate(NAMES):
        array = arrays[name]
        lead = (slice(None),) * (array.ndim - 1)
        for side, (held, first) in enumerate(((west, 0), (east, width - LANES))):
            copies.append(
                pltpu.make_async_copy(array.at[lead + (pl.ds(first, LANES),)], held[name], sems.at[number, side])
            )
    for copy in copies:
        copy.start()
    for copy in copies:
        copy.wait()
    lane = iota((rows, LANES), 1)
    for held, target, origin in ((west, to_west, 0), (east, to_east, LANES - DEEP)):
        packed = [None, None]
        for field, key in enumerate(column_fields(count)):
            side, at = group_lanes(field)
            value = masked(held, key)
            shift = (at - origin) % LANES
            if shift:
                value = pltpu.roll(value, shift, 1)
            packed[side] = value if packed[side] is None else jnp.where(lane >= at, value, packed[side])
        for side in range(2):
            target[:, side * LANES : (side + 1) * LANES] = packed[side]


def merge_rows(one, two, own_west, own_east, halo, halo_static, to_west, to_east):
    even, at_top = place()
    width = one.shape[1]
    rows = own_west.shape[0]
    count = halo.shape[0] // 3
    lane = iota((TILE, LANES), 1)
    to_west[:rows, :] = own_west[...]
    to_east[:rows, :] = own_east[...]
    packed = [[None, None], [None, None]]
    field = 0
    for key, kind, turned, at, slots in row_plan(count):
        here = slice(at, at + slots)
        north = jnp.where(even, one[here, :], two[here, :])
        south = jnp.where(even, two[here, :], one[here, :])
        blank = jnp.zeros((DEEP - slots, width), jnp.float32)
        gap = [blank] if slots < DEEP else []
        plain = jnp.concatenate([north] + gap + gap + [south], axis=0)
        values = [plain]
        if kind >= 2 and slots < DEEP:
            fold = ([north[:-1]] if slots > 1 else []) + gap + [north[-1:]] + gap + [south]
            if kind == 3:
                fold = [north[1:], blank, north[:1]] + gap + [south]
                values.append(jnp.where(at_top, jnp.concatenate(fold, axis=0), plain))
            else:
                values = [jnp.where(at_top, jnp.concatenate(fold, axis=0), plain)]
        for value in values:
            if field < halo.shape[0]:
                halo[field] = value
            else:
                halo_static[field - halo.shape[0]] = value
            side, start = group_lanes(field)
            pieces = lane_tiles(value)
            for way, piece, origin in ((0, pieces[0], 0), (1, pieces[-1], LANES - DEEP)):
                shift = (start - origin) % LANES
                if shift:
                    piece = pltpu.roll(piece, shift, 1)
                held = packed[way][side]
                packed[way][side] = piece if held is None else jnp.where(lane >= start, piece, held)
            field += 1
    halo_static[field - halo.shape[0]] = jnp.zeros((TILE, width), jnp.float32)
    for way, target in ((0, to_west), (1, to_east)):
        for side in range(2):
            target[rows:, side * LANES : (side + 1) * LANES] = packed[way][side]


def steps_kernel(
    adj_count, adj_h, adj_u, adj_v, traj_u, traj_v, wet_u, wet_v, depth, drag, land,
    halo, halo_static, from_west, from_east,
    out_h, out_u, out_v, out_depth, out_drag,
    mask_u_s, mask_v_s, keep_u_s, keep_v_s, drag_u_s, drag_v_s, vel_u_s, vel_v_s,
    depth_u_s, depth_v_s, ratio_u_s, ratio_v_s, land_s,
):
    _, at_top = place()
    rows, width = adj_h.shape[1:]
    count = rows // TILE + 1
    last = count - 1
    wide = width + LANES
    row = iota((TILE, wide), 0)
    lane = iota((TILE, LANES), 1)
    sens = pl.program_id(0)
    halo_count = 3 * adj_count

    def corner(side, at, tile):
        here = slice(tile * TILE, (tile + 1) * TILE)
        cols = slice(side * LANES, (side + 1) * LANES)
        east = pltpu.roll(from_east[here, cols], (LANES - at) % LANES, 1)
        west = pltpu.roll(from_west[here, cols], (2 * LANES - DEEP - at) % LANES, 1)
        return jnp.where(lane < LANES // 2, east, west)

    def extended(own, halo_rows, corner_of, kind):
        out = []
        for tile in range(count):
            body = own(tile) if tile < last else halo_rows()
            value = jnp.concatenate([body, corner_of(tile)], axis=1)
            if tile == last and kind == 1:
                value = jnp.where(at_top & (row < DEEP), pltpu.roll(value, wide - 1, 1), value)
            out.append(value)
        return out

    def east_of(value):
        return pltpu.roll(value, wide - 1, 1)

    def west_of(value):
        return pltpu.roll(value, 1, 1)

    def south_of(values, tile):
        return jnp.where(row == 0, pltpu.roll(values[tile - 1], 1, 0), pltpu.roll(values[tile], 1, 0))

    def north_of(values, tile):
        return jnp.where(
            row == TILE - 1,
            pltpu.roll(values[(tile + 1) % count], TILE - 1, 0),
            pltpu.roll(values[tile], TILE - 1, 0),
        )

    def rows_of(tile):
        return slice(tile * TILE, (tile + 1) * TILE)

    @pl.when(sens == 0)
    def _():
        def static(key, ref, kind):
            own = lambda tile: ref[rows_of(tile), :].astype(jnp.float32)
            if key not in TILES:
                ones = lambda columns: jnp.ones((TILE, columns), jnp.float32)
                return extended(own, lambda: ones(width), lambda tile: ones(LANES), 0)
            index = TILES.index(key)
            side, at = group_lanes(halo_count + index)
            return extended(own, lambda: halo_static[index], lambda tile: corner(side, at, tile), kind)

        cells = [jnp.where(value > 0.0, value, 1.0) for value in static(("depth", None), depth, 0)]
        drag_u = static(("drag", 1), drag, 1)
        drag_v = static(("drag", 2), drag, 2)
        sea = static(("land", None), land, 0)
        face_u = [0.5 * (value + east_of(value)) for value in cells]
        face_v = [0.5 * (cells[tile] + north_of(cells, tile)) for tile in range(count)]
        face_v[last] = jnp.where(row == 3, pltpu.roll(face_v[last - 1], DEEP, 0), face_v[last])
        for tile in range(count):
            here = rows_of(tile)
            land_s[here, :] = 0.5 * sea[tile]
            inverse_u = 1.0 / face_u[tile]
            inverse_v = 1.0 / face_v[tile]
            depth_u_s[here, :] = face_u[tile]
            depth_v_s[here, :] = face_v[tile]
            ratio_u_s[here, :] = -drag_u[tile] * inverse_u
            ratio_v_s[here, :] = -drag_v[tile] * inverse_v
        for step in range(3):
            for kind, way, vel_ref, wet_ref, depth_s, ratio_s, mask_s, keep_s, drag_s, vel_s in (
                (1, "u", traj_u, wet_u, depth_u_s, ratio_u_s, mask_u_s, keep_u_s, drag_u_s, vel_u_s),
                (2, "v", traj_v, wet_v, depth_v_s, ratio_v_s, mask_v_s, keep_v_s, drag_v_s, vel_v_s),
            ):
                vel = static(("traj_" + way, step), vel_ref.at[step], kind)
                wet = static(("wet_" + way, step), wet_ref.at[step], kind)
                for tile in range(count):
                    here = rows_of(tile)
                    square = vel[tile] * vel[tile]
                    speed = jnp.sqrt(square + speed_floor)
                    mask_s[step, here, :] = 0.5 * wet[tile]
                    keep_s[step, here, :] = 2.0 + ratio_s[here, :] * (speed + square / speed)
                    drag_s[step, here, :] = -vel[tile] * speed / depth_s[here, :]
                    vel_s[step, here, :] = vel[tile]

    def dynamic(kind, ref):
        at = DEEP * (3 * sens + kind)
        return extended(
            lambda tile: ref[0, rows_of(tile), :],
            lambda: halo[kind],
            lambda tile: corner(0, at, tile),
            kind,
        )

    bar_h, bar_u, bar_v = dynamic(0, adj_h), dynamic(1, adj_u), dynamic(2, adj_v)
    sum_xu, sum_xv, sum_u, sum_v = ([None] * count for _ in range(4))

    def add_to(sums, tile, value):
        sums[tile] = value if sums[tile] is None else sums[tile] + value

    for step in (2, 1, 0):
        flow_u, flow_v, flow_v_face, sea = [], [], [], []
        for tile in range(count):
            here = rows_of(tile)
            flow_u.append(mask_u_s[step, here, :] * bar_u[tile])
            flow_v.append(mask_v_s[step, here, :] * bar_v[tile])
        flow_v_face = list(flow_v)
        flow_v_face[last - 1] = flow_v[last - 1] - jnp.where(
            at_top & (row == TILE - 1), pltpu.roll(flow_v[last], DEEP, 0), 0.0
        )
        for tile in range(count):
            here = rows_of(tile)
            bar_h[tile] = (
                bar_h[tile]
                + (flow_u[tile] - west_of(flow_u[tile]))
                + (flow_v_face[tile] - south_of(flow_v_face, tile))
            )
            sea.append(land_s[here, :] * bar_h[tile])
        for tile in range(count):
            here = rows_of(tile)
            turn_u = east_of(sea[tile]) - sea[tile]
            turn_v = north_of(sea, tile) - sea[tile]
            if tile == last:
                turn_v = jnp.where(row == 3, -pltpu.roll(fold_turn, DEEP, 0), turn_v)
            fold_turn = turn_v
            bar_u[tile] = keep_u_s[step, here, :] * flow_u[tile] + depth_u_s[here, :] * turn_u
            bar_v[tile] = keep_v_s[step, here, :] * flow_v[tile] + depth_v_s[here, :] * turn_v
            add_to(sum_xu, tile, drag_u_s[step, here, :] * flow_u[tile])
            add_to(sum_xv, tile, drag_v_s[step, here, :] * flow_v[tile])
            add_to(sum_u, tile, vel_u_s[step, here, :] * turn_u)
            add_to(sum_v, tile, vel_v_s[step, here, :] * turn_v)

    face_v = [
        ratio_v_s[rows_of(tile), :] * sum_xv[tile] + sum_v[tile] for tile in range(count)
    ]
    for tile in range(last):
        here = rows_of(tile)
        face_u = ratio_u_s[here, :] * sum_xu[tile] + sum_u[tile]
        total = face_u + west_of(face_u) + face_v[tile] + south_of(face_v, tile)
        if tile == last - 1:
            total = total + jnp.where(
                at_top & (row == TILE - 1), pltpu.roll(face_v[last], DEEP, 0), 0.0
            )
        out_h[0, here, :] = bar_h[tile][:, :width]
        out_u[0, here, :] = bar_u[tile][:, :width]
        out_v[0, here, :] = bar_v[tile][:, :width]
        out_depth[0, here, :] = 0.5 * total[:, :width]
        out_drag[0, here, :] = (sum_xu[tile] + sum_xv[tile])[:, :width]


def on_device(traj_u, traj_v, adj_h, adj_u, adj_v, depth, drag, land, wet_u, wet_v):
    count, rows, width = adj_h.shape
    steps = traj_u.shape[0]
    args = (adj_h, adj_u, adj_v, traj_u, traj_v, wet_u, wet_v, depth, drag, land)

    def pieces(shape):
        return [pltpu.VMEM(arg.shape[:-2] + shape, arg.dtype) for arg in args] * 2

    in_place = [pl.BlockSpec(memory_space=pl.ANY)] * len(args)
    params = pltpu.CompilerParams(vmem_limit_bytes=VMEM_LIMIT)
    row_pack = jax.ShapeDtypeStruct((message_rows(count), width), jnp.float32)
    one, two = pl.pallas_call(
        pack_rows,
        in_specs=in_place,
        out_shape=[row_pack] * 2,
        scratch_shapes=pieces((TILE, width)) + [pltpu.SemaphoreType.DMA((len(args), 2))],
        compiler_params=params,
        name="pack_rows",
    )(*args)

    lons, lats, subs = (lax.axis_size(axis) for axis in GRID)
    total_rows = lats * subs

    def device(lon, row):
        return lon * total_rows + row

    one = lax.ppermute(one, "sub", [(core, core ^ 1) for core in range(subs)])
    route = []
    for lon in range(lons):
        for row in range(1, total_rows - 1, 2):
            route += [(device(lon, row), device(lon, row + 1)), (device(lon, row + 1), device(lon, row))]
        route.append((device(lon, total_rows - 1), device(lons - 1 - lon, total_rows - 1)))
    two = lax.ppermute(two, GRID, route)

    own_pack = jax.ShapeDtypeStruct((rows, 2 * LANES), jnp.float32)
    own_west, own_east = pl.pallas_call(
        pack_columns_own,
        in_specs=in_place,
        out_shape=[own_pack] * 2,
        scratch_shapes=pieces((rows, LANES)) + [pltpu.SemaphoreType.DMA((len(args), 2))],
        compiler_params=params,
        name="pack_columns",
    )(*args)

    full_pack = jax.ShapeDtypeStruct((rows + TILE, 2 * LANES), jnp.float32)
    halo, halo_static, to_west, to_east = pl.pallas_call(
        merge_rows,
        out_shape=[
            jax.ShapeDtypeStruct((3 * count, TILE, width), jnp.float32),
            jax.ShapeDtypeStruct((len(TILES), TILE, width), jnp.float32),
            full_pack,
            full_pack,
        ],
        compiler_params=params,
        name="merge_rows",
    )(one, two, own_west, own_east)
    from_east = lax.ppermute(to_west, "lon", [(lon, (lon - 1) % lons) for lon in range(lons)])
    from_west = lax.ppermute(to_east, "lon", [(lon, (lon + 1) % lons) for lon in range(lons)])

    def whole(shape):
        return pl.BlockSpec(shape, lambda sens: (0,) * len(shape))

    block = pl.BlockSpec((1, rows, width), lambda sens: (sens, 0, 0))
    out = jax.ShapeDtypeStruct(adj_h.shape, jnp.float32)
    ext = (rows + TILE, width + LANES)
    return pl.pallas_call(
        functools.partial(steps_kernel, count),
        grid=(count,),
        in_specs=[block] * 3
        + [whole(arg.shape) for arg in args[3:]]
        + [
            pl.BlockSpec((3, TILE, width), lambda sens: (sens, 0, 0)),
            pl.BlockSpec((len(TILES), TILE, width), lambda sens: (0, 0, 0)),
            whole(full_pack.shape),
            whole(full_pack.shape),
        ],
        out_specs=[block] * 5,
        out_shape=[out] * 5,
        scratch_shapes=[pltpu.VMEM((steps,) + ext, jnp.float32)] * 8 + [pltpu.VMEM(ext, jnp.float32)] * 5,
        compiler_params=params,
        name="reverse_steps",
    )(*args, halo, halo_static, from_west, from_east)


def solution(mesh):
    state = P("case", ROWS, "lon")
    fixed = P(ROWS, "lon")
    return jax.shard_map(
        on_device,
        mesh=mesh,
        in_specs=(state,) * 5 + (fixed,) * 3 + (state,) * 2,
        out_specs=(state,) * 5,
        check_vma=False,
    )
```

time: 33.8 us -> 32.7 us (0.967)
  waiting for transfers between devices: 6.46 us -> 4.4 us
  Pallas kernels: 7.64 us -> 8.62 us
    ppermute x1, waiting for transfers between devices: 4.09 us -> 2.65 us  [on_device(): two = lax.ppermute(two, GRID, route)]
    ppermute x1, starting transfers between devices: 0.48 us -> 1.54 us  [on_device(): lax.ppermute(to_west, 'lon', [(lon, (lon - 1) % lons) for lon in range(lo...]
    ppermute x1, starting transfers between devices: 2.89 us -> 1.83 us  [on_device(): lax.ppermute(to_east, 'lon', [(lon, (lon + 1) % lons) for lon in range(lo...]
    pallas_call x3, Pallas kernels: 7.48 us -> 8.41 us  [the longest x1 6.63 us: on_device(): pl.pallas_call(functools.partial(steps_kernel, count), grid=(count,), in_...]
    ppermute x1, waiting for transfers between devices: 0.93 us -> 0.27 us  [on_device(): lax.ppermute(to_west, 'lon', [(lon, (lon - 1) % lons) for lon in range(lo...]
  transfers between devices with their start and end apart: 4 -> 4, of which waited for: 3 -> 3; matrix products, arithmetic and copies ran while one was open for 0% -> 0% of each run, Pallas kernels for 1% -> 2%
where the time goes in v2:
time: 32.7 us; the launch traced here: 32.2 us
  local copies, waits for them, and re-layouts  9.36 us (29%)
  starting transfers between devices  9.11 us (28%)
  Pallas kernels  8.62 us (26%)
  waiting for transfers between devices  4.4 us (13%)
  between operations  0.72 us (2%)
    unnamed x26, local copies, waits for them, and re-layouts  9.36 us
    pallas_call x1, Pallas kernels, on_device(): pl.pallas_call(functools.partial(steps_kernel, count), grid=(count,), in_...  6.63 us
    ppermute x1, starting transfers between devices, on_device(): two = lax.ppermute(two, GRID, route)  5.22 us
    ppermute x1, waiting for transfers between devices, on_device(): two = lax.ppermute(two, GRID, route)  2.65 us
    ppermute x1, starting transfers between devices, on_device(): lax.ppermute(to_east, 'lon', [(lon, (lon + 1) % lons) for lon in range(lo...  1.83 us
    ppermute x1, starting transfers between devices, on_device(): lax.ppermute(to_west, 'lon', [(lon, (lon - 1) % lons) for lon in range(lo...  1.54 us
    ppermute x1, waiting for transfers between devices, on_device(): lax.ppermute(to_east, 'lon', [(lon, (lon + 1) % lons) for lon in range(lo...  1.48 us
    pallas_call x1, Pallas kernels, on_device(): pl.pallas_call(pack_rows, in_specs=in_place, out_shape=[row_pack] * 2, sc...  0.99 us
  transfers between devices with their start and end apart: 4, of which 3 were waited for; matrix products, arithmetic and copies ran while one was open for 0% of the time, Pallas kernels for 2%

profile of v2, /device:TPU:3, one launch (start us, length us, event | category | flops | bytes accessed | tf_op | source)
XLA Modules:
  0.0 32.2 jit_solution(9611907199560427524)
XLA Ops:
  0.6 0.0 copy-start
  0.6 1.0 %copy-done = f32[8,32,512]{2,1,0:T(8,128)S(1)} copy-done((f32[8,32,512]{2,1,0:T(8,128)S(1)}, f32[8,32,512]{2,1,0:T(8,128)}, u32[]{:S(2)}) %copy-start) | copy-done | bytes 524312
  1.7 1.0 %copy-done.2 = f32[8,32,512]{2,1,0:T(8,128)S(1)} copy-done((f32[8,32,512]{2,1,0:T(8,128)S(1)}, f32[8,32,512]{2,1,0:T(8,128)}, u32[]{:S(2)}) %copy-start.2) | copy-done | bytes 524312
  2.7 1.0 %copy-done.4 = f32[8,32,512]{2,1,0:T(8,128)S(1)} copy-done((f32[8,32,512]{2,1,0:T(8,128)S(1)}, f32[8,32,512]{2,1,0:T(8,128)}, u32[]{:S(2)}) %copy-start.4) | copy-done | bytes 524312
  3.8 0.9 %copy-done.6 = f32[3,32,512]{2,1,0:T(8,128)S(1)} copy-done((f32[3,32,512]{2,1,0:T(8,128)S(1)}, f32[3,32,512]{2,1,0:T(8,128)}, u32[]{:S(2)}) %copy-start.6) | copy-done | bytes 196632
  4.7 0.9 %copy-done.7 = f32[3,32,512]{2,1,0:T(8,128)S(1)} copy-done((f32[3,32,512]{2,1,0:T(8,128)S(1)}, f32[3,32,512]{2,1,0:T(8,128)}, u32[]{:S(2)}) %copy-start.7) | copy-done | bytes 196632
  5.6 0.9 %copy-done.8 = s32[3,32,512]{2,1,0:T(8,128)S(1)} copy-done((s32[3,32,512]{2,1,0:T(8,128)S(1)}, s32[3,32,512]{2,1,0:T(8,128)}, u32[]{:S(2)}) %copy-start.8) | copy-done | bytes 196632
  6.5 0.9 %copy-done.9 = s32[3,32,512]{2,1,0:T(8,128)S(1)} copy-done((s32[3,32,512]{2,1,0:T(8,128)S(1)}, s32[3,32,512]{2,1,0:T(8,128)}, u32[]{:S(2)}) %copy-start.9) | copy-done | bytes 196632
  7.5 0.8 %copy-done.10 = f32[32,512]{1,0:T(8,128)S(1)} copy-done((f32[32,512]{1,0:T(8,128)S(1)}, f32[32,512]{1,0:T(8,128)}, u32[]{:S(2)}) %copy-start.10) | copy-done | bytes 65560
  8.3 0.8 %copy-done.11 = f32[32,512]{1,0:T(8,128)S(1)} copy-done((f32[32,512]{1,0:T(8,128)S(1)}, f32[32,512]{1,0:T(8,128)}, u32[]{:S(2)}) %copy-start.11) | copy-done | bytes 65560
  9.2 0.8 %copy-done.12 = s32[32,512]{1,0:T(8,128)S(1)} copy-done((s32[32,512]{1,0:T(8,128)S(1)}, s32[32,512]{1,0:T(8,128)}, u32[]{:S(2)}) %copy-start.12) | copy-done | bytes 65560
  10.0 1.0 %pack_rows.1 = (f32[112,512]{1,0:T(8,128)S(1)}, f32[112,512]{1,0:T(8,128)S(1)}) custom-call(f32[8,32,512]{2,1,0:T(8,128)S(1)} %copy-done, f32[8,32,512]{2,1,0:T(8,128)S(1)} %copy-done.2, f32[8,32,512]{2,1,0:T(8,128)S(1)} %copy-done.4, f32[3,32,512]{2,1,0:T(8,128)S(1)} %copy-done.6, f32[3,32,512]{2,1,0:T(8,128)S(1)} %copy-done.7, ...), custom_call_target="tpu_custom_call" | custom-call | tf_op jit(solution)/shard_map/pack_rows/pallas_call | solution.py:400
  11.0 0.5 %collective-permute-start = (f32[112,512]{1,0:T(8,128)S(1)}, f32[112,512]{1,0:T(8,128)S(1)}, u32[]{:S(2)}, u32[]{:S(2)}) collective-permute-start(f32[112,512]{1,0:T(8,128)S(1)} %get-tuple-element.13), channel_id=1, source_target_pairs={{0,1},{1,0},{2,3},{3,2},{4,5},{5,4},{6,7},{7,6},{8,9},{9,8},{10,11... | collective-permute-start | bytes 688136 | tf_op jit(solution)/shard_map/ppermute | solution.py:415
  11.5 5.2 %collective-permute-start.1 = (f32[112,512]{1,0:T(8,128)S(1)}, f32[112,512]{1,0:T(8,128)S(1)}, u32[]{:S(2)}, u32[]{:S(2)}) collective-permute-start(f32[112,512]{1,0:T(8,128)S(1)} %get-tuple-element.14), channel_id=1, source_target_pairs={{1,2},{2,1},{3,15},{5,6},{6,5},{7,11},{9,10},{10,9},{11,7},{13,14}... | collective-permute-start | bytes 688136 | tf_op jit(solution)/shard_map/ppermute | solution.py:421
  16.7 0.0 copy-start.3
  16.7 0.0 copy-start.5
  16.8 0.8 %pack_columns.1 = (f32[32,256]{1,0:T(8,128)S(1)}, f32[32,256]{1,0:T(8,128)S(1)}) custom-call(f32[8,32,512]{2,1,0:T(8,128)S(1)} %copy-done, f32[8,32,512]{2,1,0:T(8,128)S(1)} %copy-done.2, f32[8,32,512]{2,1,0:T(8,128)S(1)} %copy-done.4, f32[3,32,512]{2,1,0:T(8,128)S(1)} %copy-done.6, f32[3,32,512]{2,1,0:T(8,128)S(1)} %copy-done.7, ...), custom_call_target="tpu_custom_call" | custom-call | tf_op jit(solution)/shard_map/pack_columns/pallas_call | solution.py:424
  17.6 2.6 %collective-permute-done.1.two = f32[112,512]{1,0:T(8,128)S(1)} collective-permute-done((f32[112,512]{1,0:T(8,128)S(1)}, f32[112,512]{1,0:T(8,128)S(1)}, u32[]{:S(2)}, u32[]{:S(2)}) %collective-permute-start.1) | collective-permute-done | bytes 229408 | tf_op jit(solution)/shard_map/ppermute | solution.py:421
  20.2 0.2 merge_rows.1
  20.4 1.8 %collective-permute-start.2 = (f32[40,256]{1,0:T(8,128)S(1)}, f32[40,256]{1,0:T(8,128)S(1)}, u32[]{:S(2)}, u32[]{:S(2)}) collective-permute-start(f32[40,256]{1,0:T(8,128)S(1)} %get-tuple-element.19), channel_id=1, source_target_pairs={{0,4},{4,8},{8,12},{12,0},{1,5},{5,9},{9,13},{13,1},{2,6},{6,10},{... | collective-permute-start | bytes 122888 | tf_op jit(solution)/shard_map/ppermute | solution.py:446
  22.3 1.5 %collective-permute-start.3 = (f32[40,256]{1,0:T(8,128)S(1)}, f32[40,256]{1,0:T(8,128)S(1)}, u32[]{:S(2)}, u32[]{:S(2)}) collective-permute-start(f32[40,256]{1,0:T(8,128)S(1)} %get-tuple-element.20), channel_id=1, source_target_pairs={{0,12},{4,0},{8,4},{12,8},{1,13},{5,1},{9,5},{13,9},{2,14},{6,2},{... | collective-permute-start | bytes 122888 | tf_op jit(solution)/shard_map/ppermute | solution.py:445
  23.8 1.5 %collective-permute-done.2.from_west = f32[40,256]{1,0:T(8,128)S(1)} collective-permute-done((f32[40,256]{1,0:T(8,128)S(1)}, f32[40,256]{1,0:T(8,128)S(1)}, u32[]{:S(2)}, u32[]{:S(2)}) %collective-permute-start.2) | collective-permute-done | bytes 40992 | tf_op jit(solution)/shard_map/ppermute | solution.py:446
  25.3 0.3 collective-permute-done.3.from_east
  25.6 6.6 %reverse_steps.1 = (f32[8,32,512]{2,1,0:T(8,128)}, f32[8,32,512]{2,1,0:T(8,128)}, f32[8,32,512]{2,1,0:T(8,128)}, f32[8,32,512]{2,1,0:T(8,128)}, f32[8,32,512]{2,1,0:T(8,128)}) custom-call(f32[8,32,512]{2,1,0:T(8,128)S(1)} %copy-done.1, f32[8,32,512]{2,1,0:T(8,128)S(1)} %copy-done.3, f32[8,32,512]{2,1,0:T(8,128)S(1)} %copy-done.5, ...), custom_call_target="tpu_custom_call" | custom-call | tf_op jit(solution)/shard_map/reverse_steps/pallas_call | solution.py:454
  (14 shorter events, 0.0 us)
Async XLA Ops:
  0.6 1.0 %copy-start = (f32[8,32,512]{2,1,0:T(8,128)S(1)}, f32[8,32,512]{2,1,0:T(8,128)}, u32[]{:S(2)}) copy-start(f32[8,32,512]{2,1,0:T(8,128)} %adj_h.1) | copy-start | bytes 1572868
  1.7 1.0 %copy-start.2 = (f32[8,32,512]{2,1,0:T(8,128)S(1)}, f32[8,32,512]{2,1,0:T(8,128)}, u32[]{:S(2)}) copy-start(f32[8,32,512]{2,1,0:T(8,128)} %adj_u.1) | copy-start | bytes 1572868
  2.7 1.0 %copy-start.4 = (f32[8,32,512]{2,1,0:T(8,128)S(1)}, f32[8,32,512]{2,1,0:T(8,128)}, u32[]{:S(2)}) copy-start(f32[8,32,512]{2,1,0:T(8,128)} %adj_v.1) | copy-start | bytes 1572868
  3.8 0.9 %copy-start.6 = (f32[3,32,512]{2,1,0:T(8,128)S(1)}, f32[3,32,512]{2,1,0:T(8,128)}, u32[]{:S(2)}) copy-start(f32[3,32,512]{2,1,0:T(8,128)} %traj_u.1) | copy-start | bytes 589828
  4.7 0.9 %copy-start.7 = (f32[3,32,512]{2,1,0:T(8,128)S(1)}, f32[3,32,512]{2,1,0:T(8,128)}, u32[]{:S(2)}) copy-start(f32[3,32,512]{2,1,0:T(8,128)} %traj_v.1) | copy-start | bytes 589828
  5.6 0.9 %copy-start.8 = (s32[3,32,512]{2,1,0:T(8,128)S(1)}, s32[3,32,512]{2,1,0:T(8,128)}, u32[]{:S(2)}) copy-start(s32[3,32,512]{2,1,0:T(8,128)} %wet_u.1) | copy-start | bytes 589828
  6.5 0.9 %copy-start.9 = (s32[3,32,512]{2,1,0:T(8,128)S(1)}, s32[3,32,512]{2,1,0:T(8,128)}, u32[]{:S(2)}) copy-start(s32[3,32,512]{2,1,0:T(8,128)} %wet_v.1) | copy-start | bytes 589828
  7.5 0.8 %copy-start.10 = (f32[32,512]{1,0:T(8,128)S(1)}, f32[32,512]{1,0:T(8,128)}, u32[]{:S(2)}) copy-start(f32[32,512]{1,0:T(8,128)} %depth.1) | copy-start | bytes 196612
  8.3 0.8 %copy-start.11 = (f32[32,512]{1,0:T(8,128)S(1)}, f32[32,512]{1,0:T(8,128)}, u32[]{:S(2)}) copy-start(f32[32,512]{1,0:T(8,128)} %drag.1) | copy-start | bytes 196612
  9.2 0.8 %copy-start.12 = (s32[32,512]{1,0:T(8,128)S(1)}, s32[32,512]{1,0:T(8,128)}, u32[]{:S(2)}) copy-start(s32[32,512]{1,0:T(8,128)} %land.1) | copy-start | bytes 196612
  11.0 6.6 %collective-permute-start = (f32[112,512]{1,0:T(8,128)S(1)}, f32[112,512]{1,0:T(8,128)S(1)}, u32[]{:S(2)}, u32[]{:S(2)}) collective-permute-start(f32[112,512]{1,0:T(8,128)S(1)} %get-tuple-element.13), channel_id=1, source_target_pairs={{0,1},{1,0},{2,3},{3,2},{4,5},{5,4},{6,7},{7,6},{8,9},{9,8},{10,11... | collective-permute-start | bytes 688136 | tf_op jit(solution)/shard_map/ppermute | solution.py:415
  11.5 8.7 %collective-permute-start.1 = (f32[112,512]{1,0:T(8,128)S(1)}, f32[112,512]{1,0:T(8,128)S(1)}, u32[]{:S(2)}, u32[]{:S(2)}) collective-permute-start(f32[112,512]{1,0:T(8,128)S(1)} %get-tuple-element.14), channel_id=1, source_target_pairs={{1,2},{2,1},{3,15},{5,6},{6,5},{7,11},{9,10},{10,9},{11,7},{13,14}... | collective-permute-start | bytes 688136 | tf_op jit(solution)/shard_map/ppermute | solution.py:421
  16.7 8.8 %copy-start.3 = (f32[8,32,512]{2,1,0:T(8,128)S(1)}, f32[8,32,512]{2,1,0:T(8,128)}, u32[]{:S(2)}) copy-start(f32[8,32,512]{2,1,0:T(8,128)} %adj_u.1) | copy-start | bytes 1572868
  16.7 8.8 %copy-start.5 = (f32[8,32,512]{2,1,0:T(8,128)S(1)}, f32[8,32,512]{2,1,0:T(8,128)}, u32[]{:S(2)}) copy-start(f32[8,32,512]{2,1,0:T(8,128)} %adj_v.1) | copy-start | bytes 1572868
  17.6 8.0 %copy-start.1 = (f32[8,32,512]{2,1,0:T(8,128)S(1)}, f32[8,32,512]{2,1,0:T(8,128)}, u32[]{:S(2)}) copy-start(f32[8,32,512]{2,1,0:T(8,128)} %adj_h.1) | copy-start | bytes 1572868
  20.4 4.9 %collective-permute-start.2 = (f32[40,256]{1,0:T(8,128)S(1)}, f32[40,256]{1,0:T(8,128)S(1)}, u32[]{:S(2)}, u32[]{:S(2)}) collective-permute-start(f32[40,256]{1,0:T(8,128)S(1)} %get-tuple-element.19), channel_id=1, source_target_pairs={{0,4},{4,8},{8,12},{12,0},{1,5},{5,9},{9,13},{13,1},{2,6},{6,10},{... | collective-permute-start | bytes 122888 | tf_op jit(solution)/shard_map/ppermute | solution.py:446
  22.3 3.3 %collective-permute-start.3 = (f32[40,256]{1,0:T(8,128)S(1)}, f32[40,256]{1,0:T(8,128)S(1)}, u32[]{:S(2)}, u32[]{:S(2)}) collective-permute-start(f32[40,256]{1,0:T(8,128)S(1)} %get-tuple-element.20), channel_id=1, source_target_pairs={{0,12},{4,0},{8,4},{12,8},{1,13},{5,1},{9,5},{13,9},{2,14},{6,2},{... | collective-permute-start | bytes 122888 | tf_op jit(solution)/shard_map/ppermute | solution.py:445
